TPU v7x, 32 devices: a whole 2x2x4 slice. The times are simulated.
32 devices in a mesh: rep: 2 (over x), shard: 4 (over y, core), head: 4 (over z).
Axes of the slice: x: 2, y: 2, z: 4, core: 2. Of those that a mesh axis runs over, the one named last changes fastest.
Arguments:
- tokens: bfloat16 [8192, 1024], P(('rep', 'shard', 'head')), may hold values from -6 to 6
- ln1_gain: bfloat16 [1024], P('shard'), may hold values from 0.25 to 1.75
- ln1_bias: bfloat16 [1024], P('shard'), may hold values from -3 to 3
- w_query: bfloat16 [1024, 1024], P('shard', 'head'), may hold values from -0.1875 to 0.1875
- w_key: bfloat16 [1024, 1024], P('shard', 'head'), may hold values from -0.1875 to 0.1875
- w_value: bfloat16 [1024, 1024], P('shard', 'head'), may hold values from -0.1875 to 0.1875
- b_query: bfloat16 [16, 64], P('head', 'shard'), may hold values from -4 to 4
- b_value: bfloat16 [16, 64], P('head', 'shard'), may hold values from -4 to 4
- w_out: bfloat16 [1024, 1024], P('head', 'shard'), may hold values from -0.75 to 0.75
- b_out: bfloat16 [1024], P('shard'), may hold values from -3 to 3
- ln2_gain: bfloat16 [1024], P('shard'), may hold values from 0.25 to 1.75
- ln2_bias: bfloat16 [1024], P('shard'), may hold values from -3 to 3
- w_up: bfloat16 [1024, 4096], P('shard', 'head'), may hold values from -0.1875 to 0.1875
- b_up: bfloat16 [32, 128], P('head', 'shard'), may hold values from -4 to 4
- w_down: bfloat16 [4096, 1024], P('head', 'shard'), may hold values from -0.125 to 0.125
- b_down: bfloat16 [1024], P('shard'), may hold values from -3 to 3
- cotangent: bfloat16 [8192, 1024], P(('rep', 'shard', 'head')), may hold values from -6 to 6
Outputs:
- output: bfloat16 [8192, 1024], P(('rep', 'shard', 'head'))
- input_grad: bfloat16 [8192, 1024], P(('rep', 'shard', 'head'))
- ln1_gain_grad: float32 [1024], P('shard')
- ln1_bias_grad: float32 [1024], P('shard')
- w_query_grad: float32 [1024, 1024], P('shard', 'head')
- w_key_grad: float32 [1024, 1024], P('shard', 'head')
- w_value_grad: float32 [1024, 1024], P('shard', 'head')
- b_query_grad: float32 [16, 64], P('head', 'shard')
- b_value_grad: float32 [16, 64], P('head', 'shard')
- w_out_grad: float32 [1024, 1024], P('head', 'shard')
- b_out_grad: float32 [1024], P('shard')
- ln2_gain_grad: float32 [1024], P('shard')
- ln2_bias_grad: float32 [1024], P('shard')
- w_up_grad: float32 [1024, 4096], P('shard', 'head')
- b_up_grad: float32 [32, 128], P('head', 'shard')
- w_down_grad: float32 [4096, 1024], P('head', 'shard')
- b_down_grad: float32 [1024], P('shard')
All inputs are finite; a program needn't handle non-finite values.
Results may differ from a plain program's by a relative error of at most 0.02.
Values may be sent and summed in bfloat16 or wider, within the bound.
A program may use at most 128 MiB of HBM per device.

v0:
```python
from functools import partial

import jax
import jax.numpy as jnp
from jax import lax
from jax.sharding import PartitionSpec as P

HEADS = 16
HD = 64
SEQ = 1024


def contract(left, right, left_dim, right_dim):
    return lax.dot_general(
        left, right, (((left_dim,), (right_dim,)), ((), ())), preferred_element_type=jnp.float32
    )


def layer_norm(rows, gain, bias):
    mean = jnp.mean(rows, axis=-1, keepdims=True)
    centred = rows - mean
    spread = jnp.mean(centred * centred, axis=-1, keepdims=True)
    return centred * lax.rsqrt(spread + 1e-05) * gain + bias


def fetch_attention(gain, shift, query_w, key_w, value_w, query_b, value_b, out_w, out_b):
    return (
        lax.all_gather(gain, "shard", axis=0, tiled=True),
        lax.all_gather(shift, "shard", axis=0, tiled=True),
        lax.all_gather(query_w, "shard", axis=0, tiled=True),
        lax.all_gather(key_w, "shard", axis=0, tiled=True),
        lax.all_gather(value_w, "shard", axis=0, tiled=True),
        lax.all_gather(query_b, "shard", axis=1, tiled=True),
        lax.all_gather(value_b, "shard", axis=1, tiled=True),
        lax.all_gather(out_w, "shard", axis=1, tiled=True),
        lax.all_gather(out_b, "shard", axis=0, tiled=True),
    )


def fetch_mlp(gain, shift, up_w, up_b, down_w, down_b):
    return (
        lax.all_gather(gain, "shard", axis=0, tiled=True),
        lax.all_gather(shift, "shard", axis=0, tiled=True),
        lax.all_gather(up_w, "shard", axis=0, tiled=True),
        lax.all_gather(up_b, "shard", axis=1, tiled=True),
        lax.all_gather(down_w, "shard", axis=1, tiled=True),
        lax.all_gather(down_b, "shard", axis=0, tiled=True),
    )


def gather_rows(normed):
    return lax.all_gather(normed, "head", axis=0, tiled=True)


def spread_grads(grads):
    return lax.all_gather(grads, "head", axis=0, tiled=True)


def branch_sum(left, right):
    return lax.psum_scatter(
        jnp.dot(left, right, preferred_element_type=jnp.float32).astype(jnp.bfloat16),
        "head",
        scatter_dimension=0,
        tiled=True,
    ).astype(jnp.float32)


def row_grads(pairs):
    total = None
    for grad, weight in pairs:
        piece = contract(grad, weight, 1, 1)
        total = piece if total is None else total + piece
    return lax.psum_scatter(
        total.astype(jnp.bfloat16), "head", scatter_dimension=0, tiled=True
    ).astype(jnp.float32)


def block_scores(queries, keys, slopes, start, block, scale):
    query_block = lax.dynamic_slice_in_dim(queries, start, block, 0)
    scores = (
        jnp.einsum("qhd,khd->hqk", query_block, keys, preferred_element_type=jnp.float32) * scale
    )
    later = start + jnp.arange(block, dtype=jnp.int32)
    earlier = jnp.arange(keys.shape[0], dtype=jnp.int32)
    distance = (later[:, None] - earlier[None, :]).astype(jnp.float32)
    scores = scores - slopes[:, None, None] * distance
    return (query_block, jnp.where(distance >= 0, scores, -1e30))


def attend(queries, keys, values, slopes, block):
    scale = queries.shape[2] ** (-0.5)

    def forward_block(index):
        query_block, scores = block_scores(queries, keys, slopes, index * block, block, scale)
        top = jnp.max(scores, axis=-1, keepdims=True)
        expo = jnp.exp(scores - top)
        total = jnp.sum(expo, axis=-1, keepdims=True)
        weights = (expo / total).astype(jnp.bfloat16)
        mixed = jnp.einsum("hqk,khd->qhd", weights, values, preferred_element_type=jnp.float32)
        return (mixed.astype(jnp.bfloat16), (top + jnp.log(total))[:, :, 0])

    count = queries.shape[0] // block
    mixed, logsum = lax.map(forward_block, jnp.arange(count, dtype=jnp.int32))
    return (mixed.reshape(queries.shape), logsum)


def attend_back(queries, keys, values, mixed_grad, logsum, slopes, block):
    scale = queries.shape[2] ** (-0.5)

    def back_block(carry, index):
        key_grad, value_grad = carry
        start = index * block
        query_block, scores = block_scores(queries, keys, slopes, start, block, scale)
        probs = jnp.exp(scores - logsum[index][:, :, None])
        grad_block = lax.dynamic_slice_in_dim(mixed_grad, start, block, 0)
        prob_grad = jnp.einsum(
            "qhd,khd->hqk", grad_block, values, preferred_element_type=jnp.float32
        )
        inner = jnp.sum(prob_grad * probs, axis=-1, keepdims=True)
        score_grad = (probs * (prob_grad - inner)).astype(jnp.bfloat16)
        query_grad = (
            jnp.einsum("hqk,khd->qhd", score_grad, keys, preferred_element_type=jnp.float32) * scale
        )
        key_grad = (
            key_grad
            + jnp.einsum(
                "hqk,qhd->khd", score_grad, query_block, preferred_element_type=jnp.float32
            )
            * scale
        )
        value_grad = value_grad + jnp.einsum(
            "hqk,qhd->khd",
            probs.astype(jnp.bfloat16),
            grad_block,
            preferred_element_type=jnp.float32,
        )
        return ((key_grad, value_grad), query_grad.astype(jnp.bfloat16))

    count = queries.shape[0] // block
    zeros = jnp.zeros(keys.shape, jnp.float32)
    (key_grad, value_grad), query_grad = lax.scan(
        back_block, (zeros, zeros), jnp.arange(count, dtype=jnp.int32)
    )
    return (
        query_grad.reshape(queries.shape),
        key_grad.astype(jnp.bfloat16),
        value_grad.astype(jnp.bfloat16),
    )


def by_owner(grad, shards):
    return grad.reshape(shards, -1)


def by_owner_inner(grad, shards):
    return grad.reshape(grad.shape[0], shards, -1).transpose(1, 0, 2).reshape(shards, -1)


def body(
    tokens,
    ln1_gain,
    ln1_bias,
    w_query,
    w_key,
    w_value,
    b_query,
    b_value,
    w_out,
    b_out,
    ln2_gain,
    ln2_bias,
    w_up,
    b_up,
    w_down,
    b_down,
    cotangent,
):
    shards = lax.axis_size("shard")
    heads_here = b_query.shape[0]
    block = min(512, SEQ)
    inputs = tokens.astype(jnp.float32)
    gain_one, shift_one, query_w, key_w, value_w, query_b, value_b, out_w, out_b = fetch_attention(
        ln1_gain, ln1_bias, w_query, w_key, w_value, b_query, b_value, w_out, b_out
    )
    normed_one = gather_rows(
        layer_norm(inputs, gain_one.astype(jnp.float32), shift_one.astype(jnp.float32)).astype(
            jnp.bfloat16
        )
    )
    seq_len = normed_one.shape[0]
    width_here = query_w.shape[1]
    queries = (
        (
            jnp.dot(normed_one, query_w, preferred_element_type=jnp.float32)
            + query_b.reshape(-1).astype(jnp.float32)
        )
        .astype(jnp.bfloat16)
        .reshape(seq_len, heads_here, HD)
    )
    keys = (
        jnp.dot(normed_one, key_w, preferred_element_type=jnp.float32)
        .astype(jnp.bfloat16)
        .reshape(seq_len, heads_here, HD)
    )
    values = (
        (
            jnp.dot(normed_one, value_w, preferred_element_type=jnp.float32)
            + value_b.reshape(-1).astype(jnp.float32)
        )
        .astype(jnp.bfloat16)
        .reshape(seq_len, heads_here, HD)
    )
    position = lax.axis_index("head") * heads_here + jnp.arange(heads_here, dtype=jnp.int32) + 1
    slopes = jnp.exp2(-8.0 * position.astype(jnp.float32) / HEADS)
    mixed, logsum = attend(queries, keys, values, slopes, block)
    mixed_rows = mixed.reshape(seq_len, width_here)
    resid = inputs + branch_sum(mixed_rows, out_w) + out_b.astype(jnp.float32)
    gain_two, shift_two, up_w, up_b, down_w, down_b = fetch_mlp(
        ln2_gain, ln2_bias, w_up, b_up, w_down, b_down
    )
    normed_two = gather_rows(
        layer_norm(resid, gain_two.astype(jnp.float32), shift_two.astype(jnp.float32)).astype(
            jnp.bfloat16
        )
    )
    hidden_pre = jnp.dot(normed_two, up_w, preferred_element_type=jnp.float32) + up_b.reshape(
        -1
    ).astype(jnp.float32)
    hidden = jax.nn.gelu(hidden_pre, approximate=True).astype(jnp.bfloat16)
    output = resid + branch_sum(hidden, down_w) + down_b.astype(jnp.float32)
    upstream = cotangent.astype(jnp.float32)
    attn_shards, mlp_shards, upstream, output = lax.optimization_barrier(
        (
            (ln1_gain, ln1_bias, w_query, w_key, w_value, b_query, b_value, w_out, b_out),
            (ln2_gain, ln2_bias, w_up, b_up, w_down, b_down),
            upstream,
            output,
        )
    )
    gain_one, shift_one, query_w, key_w, value_w, query_b, value_b, out_w, out_b = fetch_attention(
        *attn_shards
    )
    gain_two, shift_two, up_w, up_b, down_w, down_b = fetch_mlp(*mlp_shards)
    down_b_grad = jnp.sum(upstream, axis=0)
    mlp_grad = spread_grads(upstream.astype(jnp.bfloat16))
    hidden_grad = contract(mlp_grad, down_w, 1, 1)
    down_w_grad = contract(mlp_grad, hidden, 0, 0)
    unused, gelu_back = jax.vjp(partial(jax.nn.gelu, approximate=True), hidden_pre)
    pre_grad = gelu_back(hidden_grad)[0].astype(jnp.bfloat16)
    up_b_grad = jnp.sum(pre_grad.astype(jnp.float32), axis=0).reshape(up_b.shape[0], -1)
    up_w_grad = contract(normed_two, pre_grad, 0, 0)
    second_grad = row_grads(((pre_grad, up_w),))
    unused, norm_back = jax.vjp(
        layer_norm, resid, gain_two.astype(jnp.float32), shift_two.astype(jnp.float32)
    )
    resid_part, gain_two_grad, shift_two_grad = norm_back(second_grad)
    resid_grad = upstream + resid_part
    out_b_grad = jnp.sum(resid_grad, axis=0)
    attn_grad = spread_grads(resid_grad.astype(jnp.bfloat16))
    mixed_grad = (
        contract(attn_grad, out_w, 1, 1).astype(jnp.bfloat16).reshape(seq_len, heads_here, HD)
    )
    out_w_grad = contract(attn_grad, mixed_rows, 0, 0)
    query_grad, key_grad, value_grad = attend_back(
        queries, keys, values, mixed_grad, logsum, slopes, block
    )
    query_grad = query_grad.reshape(seq_len, width_here)
    key_grad = key_grad.reshape(seq_len, width_here)
    value_grad = value_grad.reshape(seq_len, width_here)
    query_b_grad = jnp.sum(query_grad.astype(jnp.float32), axis=0).reshape(heads_here, HD)
    value_b_grad = jnp.sum(value_grad.astype(jnp.float32), axis=0).reshape(heads_here, HD)
    query_w_grad = contract(normed_one, query_grad, 0, 0)
    key_w_grad = contract(normed_one, key_grad, 0, 0)
    value_w_grad = contract(normed_one, value_grad, 0, 0)
    first_grad = row_grads(((query_grad, query_w), (key_grad, key_w), (value_grad, value_w)))
    unused, first_back = jax.vjp(
        layer_norm, inputs, gain_one.astype(jnp.float32), shift_one.astype(jnp.float32)
    )
    input_part, gain_one_grad, shift_one_grad = first_back(first_grad)
    input_grad = resid_grad + input_part
    stats = jnp.stack(
        [gain_one_grad, shift_one_grad, out_b_grad, gain_two_grad, shift_two_grad, down_b_grad]
    )
    stats = lax.psum(stats, "head")
    parts = [
        by_owner(query_w_grad, shards),
        by_owner(key_w_grad, shards),
        by_owner(value_w_grad, shards),
        by_owner(out_w_grad, shards),
        by_owner(up_w_grad, shards),
        by_owner(down_w_grad, shards),
        by_owner_inner(query_b_grad, shards),
        by_owner_inner(value_b_grad, shards),
        by_owner_inner(up_b_grad, shards),
        by_owner_inner(stats, shards),
    ]
    widths = [piece.shape[1] for piece in parts]
    packed = jnp.concatenate(parts, axis=1)
    owned = lax.psum_scatter(
        packed.astype(jnp.bfloat16), "shard", scatter_dimension=0, tiled=True
    ).astype(jnp.float32)
    owned = lax.psum(owned.astype(jnp.bfloat16), "rep").astype(jnp.float32)
    owned = owned.reshape(-1)
    segments = []
    offset = 0
    for width in widths:
        segments.append(owned[offset : offset + width])
        offset = offset + width
    ffn_here = up_w.shape[1]
    query_w_out = segments[0].reshape(-1, width_here)
    key_w_out = segments[1].reshape(-1, width_here)
    value_w_out = segments[2].reshape(-1, width_here)
    out_w_out = segments[3].reshape(-1, width_here).T
    up_w_out = segments[4].reshape(-1, ffn_here)
    down_w_out = segments[5].reshape(-1, ffn_here).T
    query_b_out = segments[6].reshape(heads_here, -1)
    value_b_out = segments[7].reshape(heads_here, -1)
    up_b_out = segments[8].reshape(up_b.shape[0], -1)
    stats_out = segments[9].reshape(6, -1)
    return (
        output.astype(jnp.bfloat16),
        input_grad.astype(jnp.bfloat16),
        stats_out[0],
        stats_out[1],
        query_w_out,
        key_w_out,
        value_w_out,
        query_b_out,
        value_b_out,
        out_w_out,
        stats_out[2],
        stats_out[3],
        stats_out[4],
        up_w_out,
        up_b_out,
        down_w_out,
        stats_out[5],
    )


def solution(mesh):
    return jax.shard_map(
        body,
        mesh=mesh,
        in_specs=(
            P(("rep", "shard", "head"), None),
            P("shard"),
            P("shard"),
            P("shard", "head"),
            P("shard", "head"),
            P("shard", "head"),
            P("head", "shard"),
            P("head", "shard"),
            P("head", "shard"),
            P("shard"),
            P("shard"),
            P("shard"),
            P("shard", "head"),
            P("head", "shard"),
            P("head", "shard"),
            P("shard"),
            P(("rep", "shard", "head"), None),
        ),
        out_specs=(
            P(("rep", "shard", "head"), None),
            P(("rep", "shard", "head"), None),
            P("shard"),
            P("shard"),
            P("shard", "head"),
            P("shard", "head"),
            P("shard", "head"),
            P("head", "shard"),
            P("head", "shard"),
            P("head", "shard"),
            P("shard"),
            P("shard"),
            P("shard"),
            P("shard", "head"),
            P("head", "shard"),
            P("head", "shard"),
            P("shard"),
        ),
        check_vma=False,
    )
```

profile of v0, /device:TPU:0, one launch (start us, length us, event | category | flops | bytes accessed | tf_op | source)
XLA Modules:
  0.0 859.6 jit_solution(5853213444406843766)
XLA Ops:
  12.5 6.0 all-gather.1
  37.0 7.6 all_gather.84
  44.6 7.5 all_gather.86
  52.1 7.5 all_gather.87
  59.6 7.3 all_gather.89
  66.9 6.7 all-gather.20.cloned.1.call-done
  80.1 24.4 %while.28 = (s32[]{:T(128)}, bf16[2,512,4,64]{1,3,2,0:T(8,128)(2,1)S(1)}, f32[2,4,512]{2,1,0:T(4,128)S(1)}, s32[2]{0:T(128)S(1)}, bf16[1024,4,64]{0,2,1:T(8,128)...) while((s32[]{:T(128)}, ...), condition=%wide.region_5.6_spmd.clone, body=%wide.region_2.5_spmd.clone.sunk | while | flops 577370624 | bytes 37297388 | solution.py:103
  123.4 26.9 %reduce-scatter.5.cloned.1.call-done = bf16[256,1024]{1,0:T(8,128)(2,1)} async-done(((bf16[1024,1024]{1,0:T(8,128)(2,1)}), bf16[256,1024]{1,0:T(8,128)(2,1)}) %reduce-scatter.5.cloned.1.call-update) | async-done | bytes 524304 | tf_op jit(solution)/shard_map/reduce_scatter | solution.py:60
  161.6 38.6 %all-gather.22.cloned.1.call-done = bf16[1024,1024]{1,0:T(8,128)(2,1)} async-done(((bf16[256,1024]{1,0:T(8,128)(2,1)}), bf16[1024,1024]{1,0:T(8,128)(2,1)}) %all-gather.22.cloned.1.call-update) | async-done | bytes 2097168 | tf_op jit(solution)/shard_map/all_gather | solution.py:52
  200.1 6.5 fusion.73
  206.6 16.5 %all-gather.26.cloned.1.call-done = bf16[1024,1024]{1,0:T(8,128)(2,1)} async-done(((bf16[1024,256]{1,0:T(8,128)(2,1)}), bf16[1024,1024]{1,0:T(8,128)(2,1)}) %all-gather.26.cloned.1.call-update) | async-done | bytes 2097168 | tf_op jit(solution)/shard_map/all_gather | solution.py:46
  223.1 7.1 convolution_convert_fusion.3
  235.6 38.7 %reduce-scatter.7.cloned.1.call-done = bf16[256,1024]{1,0:T(8,128)(2,1)} async-done(((bf16[1024,1024]{1,0:T(8,128)(2,1)}), bf16[256,1024]{1,0:T(8,128)(2,1)}) %reduce-scatter.7.cloned.1.call-update) | async-done | bytes 524304 | tf_op jit(solution)/shard_map/reduce_scatter | solution.py:60
  278.2 20.4 %all-gather.30.cloned.1.call-done = bf16[1024,1024]{1,0:T(8,128)(2,1)} async-done(((bf16[1024,256]{1,0:T(8,128)(2,1)}), bf16[1024,1024]{1,0:T(8,128)(2,1)}) %all-gather.30.cloned.1.call-update) | async-done | bytes 2097168 | tf_op jit(solution)/shard_map/all_gather | solution.py:46
  298.6 47.8 %all-gather.28.cloned.1.call-done = bf16[1024,1024]{1,0:T(8,128)(2,1)} async-done(((bf16[256,1024]{1,0:T(8,128)(2,1)}), bf16[1024,1024]{1,0:T(8,128)(2,1)}) %all-gather.28.cloned.1.call-update) | async-done | bytes 2097168 | tf_op jit(solution)/shard_map/all_gather | solution.py:56
  346.3 10.2 %fusion.69 = (bf16[1024]{0:T(1024)(128)(2,1)}, bf16[1024,1024]{1,0:T(8,128)(2,1)}) fusion(f32[1024,1024]{1,0:T(8,128)} %fusion.73, f32[1024]{0:T(1024)S(1)} %bitcast.210, bf16[1024,1024]{1,0:T(8,128)(2,1)} %all-gather.28.cloned.1.call-done, bf16[1024,1024]{1,0:T(8,128)(2,1)} %all-gather.30.cloned.1.call-done), kind=kOutput, calls=%fused_computation.140 | convolution fusion | flops 2170551296 | bytes 10491904 | tf_op jit(solution)/shard_map/dot_general | solution.py:14
  356.5 12.7 %all-gather.32.cloned.1.call-done = bf16[1024,1024]{1,0:T(8,128)(2,1)} async-done(((bf16[256,1024]{1,0:T(8,128)(2,1)}), bf16[1024,1024]{1,0:T(8,128)(2,1)}) %all-gather.32.cloned.1.call-update) | async-done | bytes 2097168 | tf_op jit(solution)/shard_map/all_gather | solution.py:44
  380.4 38.7 %reduce-scatter.9.cloned.1.call-done = bf16[256,1024]{1,0:T(8,128)(2,1)} async-done(((bf16[1024,1024]{1,0:T(8,128)(2,1)}), bf16[256,1024]{1,0:T(8,128)(2,1)}) %reduce-scatter.9.cloned.1.call-update) | async-done | bytes 524304 | tf_op jit(solution)/shard_map/reduce_scatter | solution.py:73
  433.4 7.7 all_gather.103
  441.1 7.7 all_gather.104
  448.8 7.7 all_gather.105
  456.6 9.2 %all_gather.106 = bf16[1024,256]{1,0:T(8,128)(2,1)} all-gather(bf16[256,256]{1,0:T(8,128)(2,1)} %param.26), channel_id=1, replica_groups=mesh['rep'=2,'shard'=4,'head'=4] {'shard'}, dimensions={0}, use_global_device_ids=true | all-gather | bytes 655360 | tf_op jit(solution)/shard_map/all_gather | solution.py:32
  465.8 5.9 convolution_convert_fusion.1
  476.3 6.7 convolution_convert_fusion
  496.5 30.8 %while.29 = (s32[]{:T(128)}, f32[1024,4,64]{0,2,1:T(8,128)S(1)}, f32[1024,4,64]{0,2,1:T(8,128)S(1)}, bf16[2,512,4,64]{1,3,2,0:T(8,128)(2,1)}, s32[2]{0:T(128)S(1...) while((s32[]{:T(128)}, f32[1024,4,64]{0,2,1:T(8,128)S(1)}, ...), condition=%wide.region_15.16_spmd.clone, body=%wide.region_13.15_spmd.clone.sunk | while | flops 1369438720 | bytes 83671472 | solution.py:141
  559.0 27.7 %reduce-scatter.11.cloned.1.call-done = bf16[256,1024]{1,0:T(8,128)(2,1)} async-done(((bf16[1024,1024]{1,0:T(8,128)(2,1)}), bf16[256,1024]{1,0:T(8,128)(2,1)}) %reduce-scatter.11.cloned.1.call-update) | async-done | bytes 524304 | tf_op jit(solution)/shard_map/reduce_scatter | solution.py:73
  589.9 17.1 %psum.14 = bf16[6,1024]{1,0:T(8,128)(2,1)S(1)} all-reduce(f32[6,1024]{1,0:T(8,128)S(1)} %stack.15), channel_id=1, replica_groups=mesh['rep'=2,'shard'=4,'head'=4] {'head'}, use_global_device_ids=true, to_apply=%region_28.29 | all-reduce | flops 6144 | bytes 36864 | tf_op jit(solution)/shard_map/psum | solution.py:284
  608.4 117.6 %all-reduce.6.cloned.1.call-done = bf16[4,788352]{1,0:T(4,128)(2,1)} async-done(((bf16[4,788352]{1,0:T(4,128)(2,1)}), bf16[4,788352]{1,0:T(4,128)(2,1)}) %all-reduce.6.cloned.1.call-update) | async-done | bytes 6306832
  726.0 8.9 %constant_dynamic-slice_fusion = bf16[1,788352]{1,0:T(2,128)(2,1)} fusion(bf16[4,788352]{1,0:T(4,128)(2,1)} %all-reduce.6.cloned.1.call-done, u32[]{:T(128)} %bitcast.58), kind=kLoop, calls=%fused_computation.135 | loop fusion | bytes 3153412
  736.2 84.7 %all-reduce.4.cloned.1.call-done = bf16[1,788352]{1,0:T(2,128)(2,1)} async-done(((bf16[1,788352]{1,0:T(2,128)(2,1)}), bf16[1,788352]{1,0:T(2,128)(2,1)}) %all-reduce.4.cloned.1.call-update) | async-done | bytes 1576720 | tf_op jit(solution)/shard_map/psum | solution.py:302
  820.9 6.0 convert_element_type.223
  829.8 11.9 %slice_reduce_fusion = (f32[262144]{0:T(1024)}, f32[262144]{0:T(1024)S(1)}) fusion(f32[1,788352]{1,0:T(1,128)S(1)} %convert_element_type.223), kind=kLoop, calls=%fused_computation.102 | loop fusion | bytes 4194304 | tf_op jit(solution)/shard_map/slice | solution.py:307
  (298 shorter events, 210.0 us)
Async XLA Ops:
  8.0 51.6 %copy-start.19 = (bf16[256,256]{1,0:T(8,128)(2,1)S(1)}, bf16[256,256]{1,0:T(8,128)(2,1)}, u32[]{:S(2)}) copy-start(bf16[256,256]{1,0:T(8,128)(2,1)} %param.29) | copy-start | bytes 393220
  8.0 65.6 %all-gather.20.cloned.1.call-start = ((), (), s32[]{:S(2)}) async-start(), calls=%async_computation.4 | async-start | bytes 2621440 | tf_op jit(solution)/shard_map/all_gather | solution.py:52
  10.6 34.0 %copy-start.24 = (f32[256]{0:T(256)}, f32[256]{0:T(256)S(1)}, u32[]{:S(2)}) copy-start(f32[256]{0:T(256)S(1)} %broadcast_multiply_fusion.1) | copy-start | bytes 3076
  12.5 13.6 %copy-start.26 = (f32[256]{0:T(256)}, f32[256]{0:T(256)S(1)}, u32[]{:S(2)}) copy-start(f32[256]{0:T(256)S(1)} %fusion.65) | copy-start | bytes 3076
  26.0 124.3 %reduce-scatter.5.cloned.1.call-start = ((), (), s32[]{:S(2)}) async-start(), calls=%async_computation.5 | async-start | bytes 2621440 | tf_op jit(solution)/shard_map/reduce_scatter | solution.py:60
  104.5 47.1 %copy-start.10 = (bf16[1024,4,64]{0,2,1:T(8,128)(2,1)}, bf16[1024,4,64]{0,2,1:T(8,128)(2,1)S(1)}, u32[]{:S(2)}) copy-start(bf16[1024,4,64]{0,2,1:T(8,128)(2,1)S(1)} %get-tuple-element.555) | copy-start | bytes 1572868
  104.5 47.1 %copy-start.22 = (f32[2,4,512]{2,1,0:T(4,128)}, f32[2,4,512]{2,1,0:T(4,128)S(1)}, u32[]{:S(2)}) copy-start(f32[2,4,512]{2,1,0:T(4,128)S(1)} %get-tuple-element.491) | copy-start | bytes 49156
  104.6 45.7 %copy-start = (bf16[256,1024]{1,0:T(8,128)(2,1)S(1)}, bf16[256,1024]{1,0:T(8,128)(2,1)}, u32[]{:S(2)}) copy-start(bf16[256,1024]{1,0:T(8,128)(2,1)} %param.21) | copy-start | bytes 1572868
  107.5 48.3 %copy-start.35 = (bf16[8,32]{1,0:T(8,128)(2,1)S(1)}, bf16[8,32]{1,0:T(8,128)(2,1)}, u32[]{:S(2)}) copy-start(bf16[8,32]{1,0:T(8,128)(2,1)} %param.34) | copy-start | bytes 1540
  107.5 54.0 %all-gather.24.cloned.1.call-start = ((), (), s32[]{:S(2)}) async-start(), calls=%async_computation.7 | async-start | bytes 2621440 | tf_op jit(solution)/shard_map/all_gather | solution.py:44
  108.1 92.0 %all-gather.22.cloned.1.call-start = ((), (), s32[]{:S(2)}) async-start(), calls=%async_computation.6 | async-start | bytes 2621440 | tf_op jit(solution)/shard_map/all_gather | solution.py:52
  155.2 67.9 %all-gather.26.cloned.1.call-start = ((), (), s32[]{:S(2)}) async-start(), calls=%async_computation.8 | async-start | bytes 2621440 | tf_op jit(solution)/shard_map/all_gather | solution.py:46
  155.8 118.5 %reduce-scatter.7.cloned.1.call-start = ((), (), s32[]{:S(2)}) async-start(), calls=%async_computation.9 | async-start | bytes 2621440 | tf_op jit(solution)/shard_map/reduce_scatter | solution.py:60
  161.5 184.8 %copy-start.33 = (f32[128,8]{0,1:T(8,128)}, f32[128,8]{0,1:T(8,128)S(1)}, u32[]{:S(2)}) copy-start(f32[128,8]{0,1:T(8,128)S(1)} %reshape.403) | copy-start | bytes 12292
  223.1 51.2 %copy-start.1 = (bf16[256,1024]{1,0:T(8,128)(2,1)S(1)}, bf16[256,1024]{1,0:T(8,128)(2,1)}, u32[]{:S(2)}) copy-start(bf16[256,1024]{1,0:T(8,128)(2,1)} %reduce-scatter.5.cloned.1.call-done) | copy-start | bytes 1572868
  230.3 68.3 %all-gather.30.cloned.1.call-start = ((), (), s32[]{:S(2)}) async-start(), calls=%async_computation.11 | async-start | bytes 2621440 | tf_op jit(solution)/shard_map/all_gather | solution.py:46
  276.4 69.9 %all-gather.28.cloned.1.call-start = ((), (), s32[]{:S(2)}) async-start(), calls=%async_computation.10 | async-start | bytes 2621440 | tf_op jit(solution)/shard_map/all_gather | solution.py:56
  277.4 91.8 %all-gather.32.cloned.1.call-start = ((), (), s32[]{:S(2)}) async-start(), calls=%async_computation.12 | async-start | bytes 2621440 | tf_op jit(solution)/shard_map/all_gather | solution.py:44
  278.1 141.0 %reduce-scatter.9.cloned.1.call-start = ((), (), s32[]{:S(2)}) async-start(), calls=%async_computation.13 | async-start | bytes 2621440 | tf_op jit(solution)/shard_map/reduce_scatter | solution.py:73
  375.1 112.7 %all-gather.34.cloned.1.call-start = ((), (), s32[]{:S(2)}) async-start(), calls=%async_computation.14 | async-start | bytes 2621440 | tf_op jit(solution)/shard_map/all_gather | solution.py:56
  421.2 19.9 %copy-start.20 = (bf16[256,256]{1,0:T(8,128)(2,1)S(1)}, bf16[256,256]{1,0:T(8,128)(2,1)}, u32[]{:S(2)}) copy-start(bf16[256,256]{1,0:T(8,128)(2,1)} %param.24) | copy-start | bytes 393220
  421.2 27.6 %copy-start.21 = (bf16[256,256]{1,0:T(8,128)(2,1)S(1)}, bf16[256,256]{1,0:T(8,128)(2,1)}, u32[]{:S(2)}) copy-start(bf16[256,256]{1,0:T(8,128)(2,1)} %param.25) | copy-start | bytes 393220
  427.6 159.1 %reduce-scatter.11.cloned.1.call-start = ((), (), s32[]{:S(2)}) async-start(), calls=%async_computation.15 | async-start | bytes 2621440 | tf_op jit(solution)/shard_map/reduce_scatter | solution.py:73
  544.2 181.7 %all-reduce.6.cloned.1.call-start = ((), (), s32[]{:S(2)}) async-start(), calls=%async_computation.17 | async-start | bytes 12613632
  551.6 35.1 %copy-start.25 = (f32[256]{0:T(256)S(1)}, f32[256]{0:T(256)}, u32[]{:S(2)}) copy-start(f32[256]{0:T(256)} %copy-done.24) | copy-start | bytes 3076
  551.6 36.6 %copy-start.32 = (f32[256]{0:T(256)S(1)}, f32[256]{0:T(256)}, u32[]{:S(2)}) copy-start(f32[256]{0:T(256)} %copy-done.31) | copy-start | bytes 3076
  551.6 36.6 %copy-start.27 = (f32[256]{0:T(256)S(1)}, f32[256]{0:T(256)}, u32[]{:S(2)}) copy-start(f32[256]{0:T(256)} %copy-done.26) | copy-start | bytes 3076
  553.4 36.5 %copy-start.28 = (f32[1024]{0:T(1024)S(1)}, f32[1024]{0:T(1024)}, u32[]{:S(2)}) copy-start(f32[1024]{0:T(1024)} %get-tuple-element.265) | copy-start | bytes 12292
  553.4 36.5 %copy-start.29 = (f32[1024]{0:T(1024)S(1)}, f32[1024]{0:T(1024)}, u32[]{:S(2)}) copy-start(f32[1024]{0:T(1024)} %get-tuple-element.261) | copy-start | bytes 12292
  553.4 36.5 %copy-start.30 = (f32[1024]{0:T(1024)S(1)}, f32[1024]{0:T(1024)}, u32[]{:S(2)}) copy-start(f32[1024]{0:T(1024)} %get-tuple-element.323) | copy-start | bytes 12292
  586.7 21.0 %copy-start.44 = (u32[32]{0:T(128)S(1)}, u32[32]{0:T(128)}, u32[]{:S(2)}) copy-start(u32[32]{0:T(128)} %constant.100) | copy-start | bytes 388
  607.7 213.2 %all-reduce.4.cloned.1.call-start = ((), (), s32[]{:S(2)}) async-start(), calls=%async_computation.16 | async-start | bytes 6306816 | tf_op jit(solution)/shard_map/psum | solution.py:302
  (31 other events, 116.3 us)
Sparse Core Ops, SparseCore 0:
  26.1 47.4 all-gather.19
  107.6 42.6 reduce-scatter.4
  230.4 43.8 reduce-scatter.6
  375.2 43.8 reduce-scatter.8
  427.7 45.2 all-gather.33
  544.4 42.3 reduce-scatter.10
Sparse Core Ops, SparseCore 1:
  109.6 21.1 all-gather.23
  155.3 44.8 all-gather.21
  201.6 21.5 all-gather.25
  276.5 22.0 all-gather.29
  300.7 45.5 all-gather.27
  347.9 21.2 all-gather.31
  607.8 118.1 all-reduce.5
  735.0 85.8 all-reduce.3
where the time goes:
time: 871 us; the launch traced here: 860 us
  waiting for transfers between devices  479 us (55%)
  blocking collectives  137 us (16%)
  matrix products  101 us (12%)
  local copies, waits for them, and re-layouts  76.1 us (9%)
  other arithmetic  41.3 us (5%)
  between operations  16.5 us (2%)
    unnamed x15, waiting for transfers between devices  120 us
    psum x1, waiting for transfers between devices, body(): owned = lax.psum(owned.astype(jnp.bfloat16), 'rep').astype(jnp.float32)  84.7 us
    reduce_scatter x2, waiting for transfers between devices, row_grads(): lax.psum_scatter(total.astype(jnp.bfloat16), 'head', scatter_dimension=0,...  66.4 us
    reduce_scatter x2, waiting for transfers between devices, branch_sum(): lax.psum_scatter(jnp.dot(left, right, preferred_element_type=jnp.float32)...  65.6 us
    all_gather x2, waiting for transfers between devices, spread_grads(): return lax.all_gather(grads, 'head', axis=0, tiled=True)  47.8 us
    all_gather x2, waiting for transfers between devices, gather_rows(): return lax.all_gather(normed, 'head', axis=0, tiled=True)  45.3 us
    dot_general x12, matrix products, contract(): lax.dot_general(left, right, (((left_dim,), (right_dim,)), ((), ())), pre...  45 us
    all_gather x2, waiting for transfers between devices, fetch_mlp(): lax.all_gather(down_w, 'shard', axis=1, tiled=True)  36.9 us
  transfers between devices with their start and end apart: 14, of which 12 were waited for; matrix products, arithmetic and copies ran while one was open for 7% of the time, Pallas kernels for 0%

commit v1 on v0

v1 whole, which is shorter than its diff:
```python
from functools import partial

import jax
import jax.numpy as jnp
from jax import lax
from jax.experimental import pallas as pl
from jax.experimental.pallas import tpu as pltpu
from jax.sharding import PartitionSpec as P

HEADS = 16
HD = 64
SEQ = 1024
BF = jnp.bfloat16
F32 = jnp.float32


def contract(left, right, left_dim, right_dim):
    return lax.dot_general(
        left, right, (((left_dim,), (right_dim,)), ((), ())), preferred_element_type=F32
    )


def layer_norm(rows, gain, bias):
    mean = jnp.mean(rows, axis=-1, keepdims=True)
    centred = rows - mean
    spread = jnp.mean(centred * centred, axis=-1, keepdims=True)
    return centred * lax.rsqrt(spread + 1e-05) * gain + bias


def swap(value, axis, bit):
    size = lax.axis_size(axis)
    return lax.ppermute(value, axis, [(at, at ^ bit) for at in range(size)])


def spread_blocks(own):
    beside = swap(own, "shard", 1)
    across = swap(own, "shard", 2)
    corner = swap(across, "shard", 1)
    return jnp.concatenate([own, across, beside, corner], axis=0)


def blocks_by_xor(value, shard, axis):
    width = value.shape[axis] // 4
    low_bit = lax.rem(shard, 2) == 1
    high_bit = shard >= 2
    parts = [lax.slice_in_dim(value, at * width, (at + 1) * width, axis=axis) for at in range(4)]
    a, b, c, d = parts
    a, b, c, d = (
        jnp.where(low_bit, b, a), jnp.where(low_bit, a, b),
        jnp.where(low_bit, d, c), jnp.where(low_bit, c, d),
    )
    a, b, c, d = (
        jnp.where(high_bit, c, a), jnp.where(high_bit, d, b),
        jnp.where(high_bit, a, c), jnp.where(high_bit, b, d),
    )
    return jnp.concatenate([a, c, b, d], axis=axis)


def blocks_back(value, shard, axis):
    width = value.shape[axis] // 4
    a, c, b, d = [
        lax.slice_in_dim(value, at * width, (at + 1) * width, axis=axis) for at in range(4)
    ]
    low_bit = lax.rem(shard, 2) == 1
    high_bit = shard >= 2
    a, b, c, d = (
        jnp.where(high_bit, c, a), jnp.where(high_bit, d, b),
        jnp.where(high_bit, a, c), jnp.where(high_bit, b, d),
    )
    a, b, c, d = (
        jnp.where(low_bit, b, a), jnp.where(low_bit, a, b),
        jnp.where(low_bit, d, c), jnp.where(low_bit, c, d),
    )
    return jnp.concatenate([a, b, c, d], axis=axis)


def gather_rows(own):
    size = lax.axis_size("head")
    pieces = [own]
    for step in range(1, size):
        pieces.append(lax.ppermute(own, "head", [(at, (at - step) % size) for at in range(size)]))
    return jnp.concatenate(pieces, axis=0)


def scatter_rows(total):
    size = lax.axis_size("head")
    rows = total.shape[0] // size
    out = total[:rows].astype(F32)
    for step in range(1, size):
        piece = total[step * rows : (step + 1) * rows]
        out = out + lax.ppermute(
            piece, "head", [(at, (at + step) % size) for at in range(size)]
        ).astype(F32)
    return out


def scatter_grad(grad):
    width = grad.shape[0] // 4
    near = (
        grad[: 2 * width] + swap(grad[2 * width :].astype(BF), "shard", 1).astype(F32)
    )
    own = near[:width] + swap(near[width:].astype(BF), "shard", 2).astype(F32)
    own = own.astype(BF)
    if lax.axis_size("rep") == 2:
        return own.astype(F32) + swap(own, "rep", 1).astype(F32)
    return lax.psum(own.astype(F32), "rep")


def forward_kernel(count, block, slopes, starts, q_ref, k_ref, v_ref, o_ref, lse_ref):
    pair = pl.program_id(0)
    key_at = lax.broadcasted_iota(jnp.int32, (block, block), 0)
    query_at = lax.broadcasted_iota(jnp.int32, (block, block), 1)
    gap = (query_at - key_at).astype(F32)
    seen = query_at >= key_at
    rows = [pl.ds(pl.multiple_of(starts[at], block), block) for at in range(count)]
    for head in range(2):
        lanes = pl.ds(head * HD, HD)
        slope = slopes[pair * 2 + head]
        tilt = gap * slope
        for at in range(count):
            query = q_ref[rows[at], lanes]
            tiles = []
            for to in range(at + 1):
                tile = contract(k_ref[rows[to], lanes], query, 1, 1)
                tile = tile - (tilt + slope * float((at - to) * block))
                if to == at:
                    tile = jnp.where(seen, tile, -1e30)
                tiles.append(tile)
            top = jnp.max(tiles[0], axis=0, keepdims=True)
            for tile in tiles[1:]:
                top = jnp.maximum(top, jnp.max(tile, axis=0, keepdims=True))
            tiles = [jnp.exp(tile - top) for tile in tiles]
            total = jnp.sum(tiles[0], axis=0, keepdims=True)
            for tile in tiles[1:]:
                total = total + jnp.sum(tile, axis=0, keepdims=True)
            share = 1.0 / total
            mixed = None
            for to in range(at + 1):
                piece = contract(v_ref[rows[to], lanes], (tiles[to] * share).astype(BF), 0, 0)
                mixed = piece if mixed is None else mixed + piece
            o_ref[rows[at], lanes] = mixed.T.astype(BF)
            lse_ref[0, pl.ds(head * count + at, 1), :] = top + jnp.log(total)


def backward_kernel(
    count, block, slopes, starts, q_ref, k_ref, v_ref, g_ref, lse_ref,
    dq_ref, dk_ref, dv_ref, dk_sum, dv_sum,
):
    pair = pl.program_id(0)
    key_at = lax.broadcasted_iota(jnp.int32, (block, block), 0)
    query_at = lax.broadcasted_iota(jnp.int32, (block, block), 1)
    gap = (query_at - key_at).astype(F32)
    seen = query_at >= key_at
    rows = [pl.ds(pl.multiple_of(starts[at], block), block) for at in range(count)]
    for head in range(2):
        lanes = pl.ds(head * HD, HD)
        slope = slopes[pair * 2 + head]
        tilt = gap * slope
        for at in reversed(range(count)):
            query = q_ref[rows[at], lanes]
            grad = g_ref[rows[at], lanes]
            lse = lse_ref[0, pl.ds(head * count + at, 1), :]
            probs, grads = [], []
            inner = None
            for to in range(at + 1):
                tile = contract(k_ref[rows[to], lanes], query, 1, 1)
                tile = tile - (tilt + (slope * float((at - to) * block) + lse))
                if to == at:
                    tile = jnp.where(seen, tile, -1e30)
                prob = jnp.exp(tile)
                prob_grad = contract(v_ref[rows[to], lanes], grad, 1, 1)
                part = jnp.sum(prob * prob_grad, axis=0, keepdims=True)
                inner = part if inner is None else inner + part
                probs.append(prob)
                grads.append(prob_grad)
            query_grad = None
            for to in range(at + 1):
                score_grad = (probs[to] * (grads[to] - inner)).astype(BF)
                piece = contract(k_ref[rows[to], lanes], score_grad, 0, 0)
                query_grad = piece if query_grad is None else query_grad + piece
                key_piece = contract(score_grad, query, 1, 0)
                value_piece = contract(probs[to].astype(BF), grad, 1, 0)
                span = pl.ds(to * block, block)
                if at == count - 1:
                    dk_sum[span, :] = key_piece
                    dv_sum[span, :] = value_piece
                else:
                    dk_sum[span, :] += key_piece
                    dv_sum[span, :] += value_piece
            dq_ref[rows[at], lanes] = (query_grad.T * HD**-0.5).astype(BF)
        for to in range(count):
            span = pl.ds(to * block, block)
            dk_ref[rows[to], lanes] = dk_sum[span, :].astype(BF)
            dv_ref[rows[to], lanes] = dv_sum[span, :].astype(BF)


def attend(qkv, slopes, starts, block):
    seq, width = qkv.shape[0], qkv.shape[1] // 3
    pairs, count = width // 128, seq // block

    def at(first):
        return pl.BlockSpec((seq, 128), lambda pair: (0, first * pairs + pair))

    scalar = pl.BlockSpec(memory_space=pltpu.SMEM)
    return pl.pallas_call(
        partial(forward_kernel, count, block),
        grid=(pairs,),
        in_specs=[scalar, scalar, at(0), at(1), at(2)],
        out_specs=[at(0), pl.BlockSpec((1, 2 * count, block), lambda pair: (pair, 0, 0))],
        out_shape=[
            jax.ShapeDtypeStruct((seq, width), BF),
            jax.ShapeDtypeStruct((pairs, 2 * count, block), F32),
        ],
        compiler_params=pltpu.CompilerParams(vmem_limit_bytes=32 * 2**20),
        name="attend",
    )(slopes, starts, qkv, qkv, qkv)


def attend_back(qkv, grad, logsum, slopes, starts, block):
    seq, width = grad.shape
    pairs, count = width // 128, seq // block

    def at(first):
        return pl.BlockSpec((seq, 128), lambda pair: (0, first * pairs + pair))

    scalar = pl.BlockSpec(memory_space=pltpu.SMEM)
    shape = jax.ShapeDtypeStruct((seq, width), BF)
    return pl.pallas_call(
        partial(backward_kernel, count, block),
        grid=(pairs,),
        in_specs=[
            scalar, scalar, at(0), at(1), at(2), at(0),
            pl.BlockSpec((1, 2 * count, block), lambda pair: (pair, 0, 0)),
        ],
        out_specs=[at(0), at(0), at(0)],
        out_shape=[shape, shape, shape],
        scratch_shapes=[pltpu.VMEM((seq, HD), F32), pltpu.VMEM((seq, HD), F32)],
        compiler_params=pltpu.CompilerParams(vmem_limit_bytes=32 * 2**20),
        name="attend_back",
    )(slopes, starts, qkv, qkv, qkv, grad, logsum)


def body(
    tokens,
    ln1_gain,
    ln1_bias,
    w_query,
    w_key,
    w_value,
    b_query,
    b_value,
    w_out,
    b_out,
    ln2_gain,
    ln2_bias,
    w_up,
    b_up,
    w_down,
    b_down,
    cotangent,
):
    shard = lax.axis_index("shard")
    place = lax.axis_index("head")
    group = lax.axis_size("head")
    heads_here = b_query.shape[0]
    width = w_query.shape[1]
    ffn = w_up.shape[1]
    feats = ln1_gain.shape[0]
    block = tokens.shape[0]

    attn_w = spread_blocks(jnp.concatenate([w_query, w_key, w_value, w_out.T], axis=1))
    small = jnp.concatenate(
        [ln1_gain, ln1_bias, b_out, ln2_gain, ln2_bias, b_down]
        + [b_query.reshape(-1), b_value.reshape(-1), b_up.reshape(-1)]
    )
    small = lax.all_gather(small, "shard", axis=0)
    rows6 = small[:, : 6 * feats].reshape(4, 6, feats)
    rows6 = rows6.transpose(1, 0, 2).reshape(6, 4 * feats).astype(F32)
    gain_one, shift_one, out_b, gain_two, shift_two, down_b = blocks_by_xor(rows6, shard, 1)
    at = 6 * feats
    step = b_query.size
    query_b = small[:, at : at + step].reshape(4, heads_here, -1).transpose(1, 0, 2).reshape(-1)
    at += step
    value_b = small[:, at : at + step].reshape(4, heads_here, -1).transpose(1, 0, 2).reshape(-1)
    at += step
    up_b = small[:, at:].reshape(4, b_up.shape[0], -1).transpose(1, 0, 2).reshape(-1).astype(F32)
    qkv_b = jnp.concatenate([query_b, jnp.zeros_like(query_b), value_b]).astype(F32)

    inputs = blocks_by_xor(tokens, shard, 1).astype(F32)
    cot = blocks_by_xor(cotangent, shard, 1)
    normed_one = gather_rows(layer_norm(inputs, gain_one, shift_one).astype(BF))
    up_w = spread_blocks(w_up)
    down_w = spread_blocks(w_down.T)
    mlp_grad = gather_rows(cot)

    qkv_w = attn_w[:, : 3 * width]
    out_w = attn_w[:, 3 * width :]
    factor = jnp.concatenate([jnp.full((width,), HD**-0.5, F32), jnp.ones((2 * width,), F32)])
    qkv = ((jnp.dot(normed_one, qkv_w, preferred_element_type=F32) + qkv_b) * factor).astype(BF)
    position = place * heads_here + jnp.arange(heads_here, dtype=jnp.int32) + 1
    slopes = jnp.exp2(-8.0 * position.astype(F32) / HEADS)
    starts = lax.rem(jnp.arange(group, dtype=jnp.int32) - place + group, group) * block
    mixed, logsum = attend(qkv, slopes, starts, block)
    resid = inputs + scatter_rows(contract(mixed, out_w, 1, 1).astype(BF)) + out_b
    normed_two = gather_rows(layer_norm(resid, gain_two, shift_two).astype(BF))
    hidden_pre = jnp.dot(normed_two, up_w, preferred_element_type=F32) + up_b
    hidden = jax.nn.gelu(hidden_pre, approximate=True).astype(BF)
    hidden_grad = jnp.dot(mlp_grad, down_w, preferred_element_type=F32)
    unused, gelu_back = jax.vjp(partial(jax.nn.gelu, approximate=True), hidden_pre)
    pre_grad_f = gelu_back(hidden_grad)[0]
    pre_grad = pre_grad_f.astype(BF)
    second_grad = scatter_rows(contract(pre_grad, up_w, 1, 1).astype(BF))
    output = resid + scatter_rows(contract(hidden, down_w, 1, 1).astype(BF)) + down_b
    output = blocks_back(output.astype(BF), shard, 1)
    upstream = cot.astype(F32)
    down_b_grad = jnp.sum(upstream, axis=0)
    down_w_grad = scatter_grad(contract(mlp_grad, hidden, 0, 0))
    up_w_grad = scatter_grad(contract(normed_two, pre_grad, 0, 0))
    up_b_grad = jnp.sum(pre_grad.astype(F32), axis=0)
    unused, norm_back = jax.vjp(layer_norm, resid, gain_two, shift_two)
    resid_part, gain_two_grad, shift_two_grad = norm_back(second_grad)
    resid_grad = upstream + resid_part
    out_b_grad = jnp.sum(resid_grad, axis=0)
    attn_grad = gather_rows(resid_grad.astype(BF))
    mixed_grad = jnp.dot(attn_grad, out_w, preferred_element_type=F32).astype(BF)
    out_w_grad = scatter_grad(contract(attn_grad, mixed, 0, 0))
    query_grad, key_grad, value_grad = attend_back(qkv, mixed_grad, logsum, slopes, starts, block)
    qkv_grad = jnp.concatenate([query_grad, key_grad, value_grad], axis=1)
    first_grad = scatter_rows(contract(qkv_grad, qkv_w, 1, 1).astype(BF))
    qkv_w_grad = scatter_grad(contract(normed_one, qkv_grad, 0, 0))
    query_b_grad = jnp.sum(query_grad.astype(F32), axis=0)
    value_b_grad = jnp.sum(value_grad.astype(F32), axis=0)
    unused, first_back = jax.vjp(layer_norm, inputs, gain_one, shift_one)
    input_part, gain_one_grad, shift_one_grad = first_back(first_grad)
    input_grad = blocks_back((resid_grad + input_part).astype(BF), shard, 1)

    stats = jnp.stack(
        [gain_one_grad, shift_one_grad, out_b_grad, gain_two_grad, shift_two_grad, down_b_grad]
    )
    stats = blocks_back(stats, shard, 1).reshape(-1)
    biases = jnp.concatenate([query_b_grad, value_b_grad, up_b_grad])
    mine = (jnp.arange(group, dtype=jnp.int32) == place)[:, None]
    biases = jnp.where(mine, biases[None, :], 0.0).reshape(-1)
    sums = lax.psum(jnp.concatenate([stats, biases]), ("rep", "shard", "head"))
    stats = sums[: stats.size].reshape(6, 4, feats)
    stats = lax.dynamic_index_in_dim(stats, shard, 1, keepdims=False)
    biases = lax.dynamic_index_in_dim(
        sums[6 * 4 * feats :].reshape(group, -1), place, 0, keepdims=False
    )

    def own_part(values, rows):
        parts = values.reshape(rows, 4, -1)
        return lax.dynamic_index_in_dim(parts, shard, 1, keepdims=False)

    return (
        output,
        input_grad,
        stats[0],
        stats[1],
        qkv_w_grad[:, :width],
        qkv_w_grad[:, width : 2 * width],
        qkv_w_grad[:, 2 * width :],
        own_part(biases[:width], heads_here),
        own_part(biases[width : 2 * width], heads_here),
        out_w_grad.T,
        stats[2],
        stats[3],
        stats[4],
        up_w_grad,
        own_part(biases[2 * width :], b_up.shape[0]),
        down_w_grad.T,
        stats[5],
    )


def solution(mesh):
    return jax.shard_map(
        body,
        mesh=mesh,
        in_specs=(
            P(("rep", "shard", "head"), None),
            P("shard"),
            P("shard"),
            P("shard", "head"),
            P("shard", "head"),
            P("shard", "head"),
            P("head", "shard"),
            P("head", "shard"),
            P("head", "shard"),
            P("shard"),
            P("shard"),
            P("shard"),
            P("shard", "head"),
            P("head", "shard"),
            P("head", "shard"),
            P("shard"),
            P(("rep", "shard", "head"), None),
        ),
        out_specs=(
            P(("rep", "shard", "head"), None),
            P(("rep", "shard", "head"), None),
            P("shard"),
            P("shard"),
            P("shard", "head"),
            P("shard", "head"),
            P("shard", "head"),
            P("head", "shard"),
            P("head", "shard"),
            P("head", "shard"),
            P("shard"),
            P("shard"),
            P("shard"),
            P("shard", "head"),
            P("head", "shard"),
            P("head", "shard"),
            P("shard"),
        ),
        check_vma=False,
    )
```

time: 871 us -> 525 us (0.60)
  waiting for transfers between devices: 479 us -> 206 us
  starting transfers between devices: 0.6 us -> 121 us
  blocking collectives: 137 us -> 46.7 us
  matrix products: 101 us -> 38.4 us
  local copies, waits for them, and re-layouts: 76.1 us -> 49.7 us
  Pallas kernels: 0 us -> 19.7 us
  between operations: 16.5 us -> 2.21 us
  other arithmetic: 41.3 us -> 31.5 us
    ppermute x0 -> x45, waiting for transfers between devices: none -> 206 us  [the longest x12 113 us: scatter_rows(): lax.ppermute(piece, 'head', [(at, (at + step) % size) for at in range(siz...]
    all_gather x8 -> x0, waiting for transfers between devices: 143 us -> none  [the longest x2 47.8 us: spread_grads(): return lax.all_gather(grads, 'head', axis=0, tiled=True)]
    reduce_scatter x4 -> x0, waiting for transfers between devices: 132 us -> none  [the longest x2 66.4 us: row_grads(): lax.psum_scatter(total.astype(jnp.bfloat16), 'head', scatter_dimension=0,...]
    ppermute x0 -> x45, starting transfers between devices: none -> 121 us  [the longest x12 60.2 us: scatter_rows(): lax.ppermute(piece, 'head', [(at, (at + step) % size) for at in range(siz...]
    unnamed x15 -> x0, waiting for transfers between devices: 120 us -> none
    all_gather x19 -> x1, blocking collectives: 120 us -> 6.79 us  [body(): small = lax.all_gather(small, 'shard', axis=0)]
    psum x1 -> x0, waiting for transfers between devices: 84.7 us -> none  [body(): owned = lax.psum(owned.astype(jnp.bfloat16), 'rep').astype(jnp.float32)]
    dot_general x20 -> x4, matrix products: 56.4 us -> 16.3 us  [the longest x1 6.18 us: body(): hidden_grad = jnp.dot(mlp_grad, down_w, preferred_element_type=F32)]
  transfers between devices with their start and end apart: 14 -> 45, of which waited for: 12 -> 15; matrix products, arithmetic and copies ran while one was open for 7% -> 19% of each run, Pallas kernels for 0% -> 4%
where the time goes in v1:
time: 525 us; the launch traced here: 516 us
  waiting for transfers between devices  206 us (39%)
  starting transfers between devices  121 us (23%)
  local copies, waits for them, and re-layouts  49.7 us (9%)
  blocking collectives  46.7 us (9%)
  matrix products  38.4 us (7%)
  other arithmetic  31.5 us (6%)
  Pallas kernels  19.7 us (4%)
    ppermute x12, waiting for transfers between devices, scatter_rows(): lax.ppermute(piece, 'head', [(at, (at + step) % size) for at in range(siz...  113 us
    ppermute x12, waiting for transfers between devices, gather_rows(): lax.ppermute(own, 'head', [(at, (at - step) % size) for at in range(size)])  85.8 us
    ppermute x12, starting transfers between devices, scatter_rows(): lax.ppermute(piece, 'head', [(at, (at + step) % size) for at in range(siz...  60.2 us
    ppermute x12, starting transfers between devices, gather_rows(): lax.ppermute(own, 'head', [(at, (at - step) % size) for at in range(size)])  43.4 us
    psum x1, blocking collectives, body(): sums = lax.psum(jnp.concatenate([stats, biases]), ('rep', 'shard', 'head'))  39.9 us
    unnamed x102, local copies, waits for them, and re-layouts  25.5 us
    dot_general x8, matrix products, contract(): lax.dot_general(left, right, (((left_dim,), (right_dim,)), ((), ())), pre...  22 us
    ppermute x21, starting transfers between devices, swap(): return lax.ppermute(value, axis, [(at, at ^ bit) for at in range(size)])  17.8 us
  transfers between devices with their start and end apart: 45, of which 15 were waited for; matrix products, arithmetic and copies ran while one was open for 19% of the time, Pallas kernels for 4%

profile of v1, /device:TPU:0, one launch (start us, length us, event | category | flops | bytes accessed | tf_op | source)
XLA Modules:
  0.0 516.1 jit_solution(8013302025643224689)
XLA Ops:
  10.8 4.1 concatenate.66
  14.9 6.8 %all-gather.1 = bf16[4,1,1920]{2,1,0:T(2,128)(2,1)S(1)} all-gather(bf16[1,1,1920]{2,1,0:T(2,128)(2,1)S(1)} %reshape.233), channel_id=2, replica_groups=mesh['rep'=2,'shard'=4,'head'=4] {'shard'}, dimensions={0}, use_global_device_ids=true | all-gather | bytes 19200 | tf_op jit(solution)/shard_map/all_gather | solution.py:276
  35.2 3.4 pad_maximum_fusion.1
  41.2 22.2 %collective-permute-done.1 = bf16[256,1024]{0,1:T(8,128)(2,1)} collective-permute-done((bf16[256,1024]{0,1:T(8,128)(2,1)S(1)}, bf16[256,1024]{0,1:T(8,128)(2,1)}, u32[]{:S(2)}, u32[]{:S(2)}) %collective-permute-start.1) | collective-permute-done | bytes 524320 | tf_op jit(solution)/shard_map/ppermute | solution.py:81
  63.4 3.4 multiply_convert_fusion.1.q_ref.k_ref.v_ref
  66.8 7.9 %attend.1 = (bf16[1024,256]{1,0:T(8,128)(2,1)S(1)}, f32[2,8,256]{2,1,0:T(8,128)S(1)}) custom-call(f32[4]{0:T(128)S(1)} %multiply_exponential_fusion.slopes, s32[4]{0:T(128)S(1)} %fusion.37.starts, bf16[1024,768]{1,0:T(8,128)(2,1)S(1)} %multiply_convert_fusion.1.q_ref.k_ref.v_ref, bf16[1024,768]{1,0:T(8,128)(2,1)S(1)} %multiply_convert_fusion.1.q_ref.k_ref.v_ref, ...), custom_call_target="tpu_custom_call" | custom-call | tf_op jit(solution)/shard_map/attend/pallas_call | solution.py:205
  78.1 12.7 %collective-permute-start.8 = (bf16[256,1024]{0,1:T(8,128)(2,1)}, bf16[256,1024]{0,1:T(8,128)(2,1)S(1)}, u32[]{:S(2)}, u32[]{:S(2)}) collective-permute-start(bf16[256,1024]{0,1:T(8,128)(2,1)} %get-tuple-element.122), channel_id=1, source_target_pairs={{0,3},{1,0},{2,1},{3,2},{4,7},{5,4},{6,5},{7,6},{8,11},{9,8},{10,9... | collective-permute-start | bytes 1572872 | tf_op jit(solution)/shard_map/ppermute | solution.py:91
  103.6 33.4 %collective-permute-done.7 = bf16[256,1024]{0,1:T(8,128)(2,1)S(1)} collective-permute-done((bf16[256,1024]{0,1:T(8,128)(2,1)}, bf16[256,1024]{0,1:T(8,128)(2,1)S(1)}, u32[]{:S(2)}, u32[]{:S(2)}) %collective-permute-start.7) | collective-permute-done | bytes 524320 | tf_op jit(solution)/shard_map/ppermute | solution.py:91
  141.6 3.4 collective-permute-start.9
  152.6 5.6 %collective-permute-done.11 = bf16[256,1024]{0,1:T(8,128)(2,1)} collective-permute-done((bf16[256,1024]{0,1:T(8,128)(2,1)}, bf16[256,1024]{0,1:T(8,128)(2,1)}, u32[]{:S(2)}, u32[]{:S(2)}) %collective-permute-start.11) | collective-permute-done | bytes 524320 | tf_op jit(solution)/shard_map/ppermute | solution.py:81
  158.2 20.6 %collective-permute-start.22 = (bf16[256,1024]{0,1:T(8,128)(2,1)S(1)}, bf16[256,1024]{0,1:T(8,128)(2,1)S(1)}, u32[]{:S(2)}, u32[]{:S(2)}) collective-permute-start(bf16[256,1024]{0,1:T(8,128)(2,1)S(1)} %pad_maximum_fusion.10), channel_id=1, source_target_pairs={{0,2},{1,3},{2,0},{3,1},{4,6},{5,7},{6,4},{7,5},{8,10},{9,11},{10,... | collective-permute-start | bytes 1572872 | tf_op jit(solution)/shard_map/ppermute | solution.py:81
  178.8 21.0 %collective-permute-done.10 = bf16[256,1024]{0,1:T(8,128)(2,1)} collective-permute-done((bf16[256,1024]{0,1:T(8,128)(2,1)}, bf16[256,1024]{0,1:T(8,128)(2,1)}, u32[]{:S(2)}, u32[]{:S(2)}) %collective-permute-start.10) | collective-permute-done | bytes 524320 | tf_op jit(solution)/shard_map/ppermute | solution.py:81
  199.7 8.5 %collective-permute-start.21 = (bf16[256,1024]{0,1:T(8,128)(2,1)S(1)}, bf16[256,1024]{0,1:T(8,128)(2,1)S(1)}, u32[]{:S(2)}, u32[]{:S(2)}) collective-permute-start(bf16[256,1024]{0,1:T(8,128)(2,1)S(1)} %pad_maximum_fusion.10), channel_id=1, source_target_pairs={{0,3},{1,0},{2,1},{3,2},{4,7},{5,4},{6,5},{7,6},{8,11},{9,8},{10,9... | collective-permute-start | bytes 1572872 | tf_op jit(solution)/shard_map/ppermute | solution.py:81
  208.3 4.7 fusion.26
  213.0 10.9 %collective-permute-done.22 = bf16[256,1024]{0,1:T(8,128)(2,1)S(1)} collective-permute-done((bf16[256,1024]{0,1:T(8,128)(2,1)S(1)}, bf16[256,1024]{0,1:T(8,128)(2,1)S(1)}, u32[]{:S(2)}, u32[]{:S(2)}) %collective-permute-start.22) | collective-permute-done | bytes 524320 | tf_op jit(solution)/shard_map/ppermute | solution.py:81
  223.9 6.2 %convert_reduce_fusion = (f32[1024]{0:T(1024)S(1)}, bf16[1024,1024]{1,0:T(8,128)(2,1)S(1)}) fusion(f32[1024,1024]{1,0:T(8,128)S(1)} %fusion.26, f32[1024]{0:T(1024)S(1)} %reshape.229, bf16[256,1024]{0,1:T(8,128)(2,1)S(1)} %collective-permute-done.17, bf16[256,1024]{0,1:T(8,128)(2,1)S(1)} %collective-permute-done.16, ...), kind=kOutput, calls=%fused_computation.9 | convolution fusion | flops 2194668544 | bytes 10493952 | tf_op jit(solution)/shard_map/dot_general | solution.py:308
  232.6 10.5 %collective-permute-start.26 = (bf16[256,1024]{0,1:T(8,128)(2,1)S(1)}, bf16[256,1024]{0,1:T(8,128)(2,1)S(1)}, u32[]{:S(2)}, u32[]{:S(2)}) collective-permute-start(bf16[256,1024]{0,1:T(8,128)(2,1)S(1)} %get-tuple-element.116), channel_id=1, source_target_pairs={{0,3},{1,0},{2,1},{3,2},{4,7},{5,4},{6,5},{7,6},{8,11},{9,8},{10,9... | collective-permute-start | bytes 1572872 | tf_op jit(solution)/shard_map/ppermute | solution.py:91
  245.0 3.8 convolution_convert_fusion.1
  248.9 3.9 collective-permute-start.20
  252.8 3.9 fusion.25
  263.6 17.2 %collective-permute-start.18 = (bf16[256,1024]{0,1:T(8,128)(2,1)S(1)}, bf16[256,1024]{0,1:T(8,128)(2,1)S(1)}, u32[]{:S(2)}, u32[]{:S(2)}) collective-permute-start(bf16[256,1024]{0,1:T(8,128)(2,1)S(1)} %get-tuple-element.118), channel_id=1, source_target_pairs={{0,1},{1,2},{2,3},{3,0},{4,5},{5,6},{6,7},{7,4},{8,9},{9,10},{10,1... | collective-permute-start | bytes 1572872 | tf_op jit(solution)/shard_map/ppermute | solution.py:91
  280.8 33.1 %collective-permute-done.25 = bf16[256,1024]{0,1:T(8,128)(2,1)S(1)} collective-permute-done((bf16[256,1024]{0,1:T(8,128)(2,1)S(1)}, bf16[256,1024]{0,1:T(8,128)(2,1)S(1)}, u32[]{:S(2)}, u32[]{:S(2)}) %collective-permute-start.25) | collective-permute-done | bytes 524320 | tf_op jit(solution)/shard_map/ppermute | solution.py:91
  315.2 19.2 %collective-permute-done.19 = bf16[256,1024]{0,1:T(8,128)(2,1)S(1)} collective-permute-done((bf16[256,1024]{0,1:T(8,128)(2,1)S(1)}, bf16[256,1024]{0,1:T(8,128)(2,1)S(1)}, u32[]{:S(2)}, u32[]{:S(2)}) %collective-permute-start.19) | collective-permute-done | bytes 524320 | tf_op jit(solution)/shard_map/ppermute | solution.py:91
  336.6 3.7 collective-permute-start.27
  349.2 3.8 collective-permute-done.29
  353.1 19.7 %collective-permute-done.28 = bf16[256,1024]{0,1:T(8,128)(2,1)} collective-permute-done((bf16[256,1024]{0,1:T(8,128)(2,1)S(1)}, bf16[256,1024]{0,1:T(8,128)(2,1)}, u32[]{:S(2)}, u32[]{:S(2)}) %collective-permute-start.28) | collective-permute-done | bytes 524320 | tf_op jit(solution)/shard_map/ppermute | solution.py:81
  374.9 11.8 %attend_back.1 = (bf16[1024,256]{1,0:T(8,128)(2,1)S(1)}, bf16[1024,256]{1,0:T(8,128)(2,1)S(1)}, bf16[1024,256]{1,0:T(8,128)(2,1)S(1)}) custom-call(f32[4]{0:T(128)S(1)} %multiply_exponential_fusion.slopes, s32[4]{0:T(128)S(1)} %fusion.37.starts, bf16[1024,768]{1,0:T(8,128)(2,1)S(1)} %multiply_convert_fusion.1.q_ref.k_ref.v_ref, ...), custom_call_target="tpu_custom_call" | custom-call | tf_op jit(solution)/shard_map/attend_back/pallas_call | solution.py:228
  390.1 12.3 %collective-permute-start.32 = (bf16[256,1024]{0,1:T(8,128)(2,1)}, bf16[256,1024]{0,1:T(8,128)(2,1)}, u32[]{:S(2)}, u32[]{:S(2)}) collective-permute-start(bf16[256,1024]{0,1:T(8,128)(2,1)} %get-tuple-element.113), channel_id=1, source_target_pairs={{0,3},{1,0},{2,1},{3,2},{4,7},{5,4},{6,5},{7,6},{8,11},{9,8},{10,9... | collective-permute-start | bytes 1572872 | tf_op jit(solution)/shard_map/ppermute | solution.py:91
  404.6 4.8 fusion.27
  422.0 25.4 %collective-permute-done.31 = bf16[256,1024]{0,1:T(8,128)(2,1)} collective-permute-done((bf16[256,1024]{0,1:T(8,128)(2,1)}, bf16[256,1024]{0,1:T(8,128)(2,1)}, u32[]{:S(2)}, u32[]{:S(2)}) %collective-permute-start.31) | collective-permute-done | bytes 524320 | tf_op jit(solution)/shard_map/ppermute | solution.py:91
  452.2 39.9 %psum.7 = f32[12288]{0:T(1024)S(1)} all-reduce(f32[12288]{0:T(1024)S(1)} %pad_maximum_fusion.22), channel_id=1, replica_groups=mesh['rep'=2,'shard'=4,'head'=4] {'rep','shard','head'}, use_global_device_ids=true, to_apply=%region_17.18 | all-reduce | flops 12288 | bytes 98304 | tf_op jit(solution)/shard_map/psum | solution.py:344
  501.2 3.5 collective-permute-done.34
  (281 shorter events, 123.0 us)
Async XLA Ops:
  26.3 37.1 %collective-permute-start.1 = (bf16[256,1024]{0,1:T(8,128)(2,1)S(1)}, bf16[256,1024]{0,1:T(8,128)(2,1)}, u32[]{:S(2)}, u32[]{:S(2)}) collective-permute-start(bf16[256,1024]{0,1:T(8,128)(2,1)S(1)} %fusion.16), channel_id=1, source_target_pairs={{0,2},{1,3},{2,0},{3,1},{4,6},{5,7},{6,4},{7,5},{8,10},{9,11},{10,... | collective-permute-start | bytes 1572872 | tf_op jit(solution)/shard_map/ppermute | solution.py:81
  28.9 34.6 %collective-permute-start = (bf16[256,1024]{0,1:T(8,128)(2,1)S(1)}, bf16[256,1024]{0,1:T(8,128)(2,1)}, u32[]{:S(2)}, u32[]{:S(2)}) collective-permute-start(bf16[256,1024]{0,1:T(8,128)(2,1)S(1)} %fusion.16), channel_id=1, source_target_pairs={{0,3},{1,0},{2,1},{3,2},{4,7},{5,4},{6,5},{7,6},{8,11},{9,8},{10,9... | collective-permute-start | bytes 1572872 | tf_op jit(solution)/shard_map/ppermute | solution.py:81
  33.4 67.1 %collective-permute-start.12 = (bf16[256,1024]{1,0:T(8,128)(2,1)}, bf16[256,1024]{1,0:T(8,128)(2,1)}, u32[]{:S(2)}, u32[]{:S(2)}) collective-permute-start(bf16[256,1024]{1,0:T(8,128)(2,1)} %param.29), channel_id=1, source_target_pairs={{0,8},{4,12},{8,0},{12,4},{1,9},{5,13},{9,1},{13,5},{2,10},{6,14},... | collective-permute-start | bytes 1572872 | tf_op jit(solution)/shard_map/ppermute | solution.py:32
  35.0 106.6 %collective-permute-start.13 = (bf16[256,1024]{1,0:T(8,128)(2,1)}, bf16[256,1024]{1,0:T(8,128)(2,1)}, u32[]{:S(2)}, u32[]{:S(2)}) collective-permute-start(bf16[256,1024]{1,0:T(8,128)(2,1)} %param.29), channel_id=1, source_target_pairs={{0,4},{4,0},{8,12},{12,8},{1,5},{5,1},{9,13},{13,9},{2,6},{6,2},{1... | collective-permute-start | bytes 1572872 | tf_op jit(solution)/shard_map/ppermute | solution.py:32
  90.9 46.2 %collective-permute-start.7 = (bf16[256,1024]{0,1:T(8,128)(2,1)}, bf16[256,1024]{0,1:T(8,128)(2,1)S(1)}, u32[]{:S(2)}, u32[]{:S(2)}) collective-permute-start(bf16[256,1024]{0,1:T(8,128)(2,1)} %get-tuple-element.123), channel_id=1, source_target_pairs={{0,2},{1,3},{2,0},{3,1},{4,6},{5,7},{6,4},{7,5},{8,10},{9,11},{10,... | collective-permute-start | bytes 1572872 | tf_op jit(solution)/shard_map/ppermute | solution.py:91
  91.3 45.8 %collective-permute-start.6 = (bf16[256,1024]{0,1:T(8,128)(2,1)}, bf16[256,1024]{0,1:T(8,128)(2,1)}, u32[]{:S(2)}, u32[]{:S(2)}) collective-permute-start(bf16[256,1024]{0,1:T(8,128)(2,1)} %get-tuple-element.121), channel_id=1, source_target_pairs={{0,1},{1,2},{2,3},{3,0},{4,5},{5,6},{6,7},{7,4},{8,9},{9,10},{10,1... | collective-permute-start | bytes 1572872 | tf_op jit(solution)/shard_map/ppermute | solution.py:91
  100.5 51.5 %collective-permute-start.15 = (bf16[256,1024]{0,1:T(8,128)(2,1)}, bf16[256,1024]{0,1:T(8,128)(2,1)}, u32[]{:S(2)}, u32[]{:S(2)}) collective-permute-start(bf16[256,1024]{0,1:T(8,128)(2,1)} %bitcast.88), channel_id=1, source_target_pairs={{0,8},{4,12},{8,0},{12,4},{1,9},{5,13},{9,1},{13,5},{2,10},{6,14},... | collective-permute-start | bytes 1572872 | tf_op jit(solution)/shard_map/ppermute | solution.py:32
  103.6 46.5 %collective-permute-start.14 = (bf16[256,1024]{1,0:T(8,128)(2,1)}, bf16[256,1024]{1,0:T(8,128)(2,1)}, u32[]{:S(2)}, u32[]{:S(2)}) collective-permute-start(bf16[256,1024]{1,0:T(8,128)(2,1)} %collective-permute-done.12), channel_id=1, source_target_pairs={{0,4},{4,0},{8,12},{12,8},{1,5},{5,1},{9,13},{13,9},{2,6},{6,2},{1... | collective-permute-start | bytes 1572872 | tf_op jit(solution)/shard_map/ppermute | solution.py:32
  141.1 58.6 %collective-permute-start.10 = (bf16[256,1024]{0,1:T(8,128)(2,1)}, bf16[256,1024]{0,1:T(8,128)(2,1)}, u32[]{:S(2)}, u32[]{:S(2)}) collective-permute-start(bf16[256,1024]{0,1:T(8,128)(2,1)} %add_convert_fusion.2), channel_id=1, source_target_pairs={{0,2},{1,3},{2,0},{3,1},{4,6},{5,7},{6,4},{7,5},{8,10},{9,11},{10,... | collective-permute-start | bytes 1572872 | tf_op jit(solution)/shard_map/ppermute | solution.py:81
  141.6 66.7 %collective-permute-start.9 = (bf16[256,1024]{0,1:T(8,128)(2,1)}, bf16[256,1024]{0,1:T(8,128)(2,1)}, u32[]{:S(2)}, u32[]{:S(2)}) collective-permute-start(bf16[256,1024]{0,1:T(8,128)(2,1)} %add_convert_fusion.2), channel_id=1, source_target_pairs={{0,3},{1,0},{2,1},{3,2},{4,7},{5,4},{6,5},{7,6},{8,11},{9,8},{10,9... | collective-permute-start | bytes 1572872 | tf_op jit(solution)/shard_map/ppermute | solution.py:81
  150.1 62.9 %collective-permute-start.16 = (bf16[256,1024]{0,1:T(8,128)(2,1)}, bf16[256,1024]{0,1:T(8,128)(2,1)S(1)}, u32[]{:S(2)}, u32[]{:S(2)}) collective-permute-start(bf16[256,1024]{0,1:T(8,128)(2,1)} %bitcast.89), channel_id=1, source_target_pairs={{0,4},{4,0},{8,12},{12,8},{1,5},{5,1},{9,13},{13,9},{2,6},{6,2},{1... | collective-permute-start | bytes 1572872 | tf_op jit(solution)/shard_map/ppermute | solution.py:32
  152.0 61.0 %collective-permute-start.23 = (bf16[256,1024]{0,1:T(8,128)(2,1)S(1)}, bf16[256,1024]{0,1:T(8,128)(2,1)S(1)}, u32[]{:S(2)}, u32[]{:S(2)}) collective-permute-start(bf16[256,1024]{0,1:T(8,128)(2,1)S(1)} %pad_maximum_fusion.10), channel_id=1, source_target_pairs={{0,1},{1,2},{2,3},{3,0},{4,5},{5,6},{6,7},{7,4},{8,9},{9,10},{10,1... | collective-permute-start | bytes 1572872 | tf_op jit(solution)/shard_map/ppermute | solution.py:81
  158.2 65.7 %collective-permute-start.22 = (bf16[256,1024]{0,1:T(8,128)(2,1)S(1)}, bf16[256,1024]{0,1:T(8,128)(2,1)S(1)}, u32[]{:S(2)}, u32[]{:S(2)}) collective-permute-start(bf16[256,1024]{0,1:T(8,128)(2,1)S(1)} %pad_maximum_fusion.10), channel_id=1, source_target_pairs={{0,2},{1,3},{2,0},{3,1},{4,6},{5,7},{6,4},{7,5},{8,10},{9,11},{10,... | collective-permute-start | bytes 1572872 | tf_op jit(solution)/shard_map/ppermute | solution.py:81
  232.6 31.0 %collective-permute-start.26 = (bf16[256,1024]{0,1:T(8,128)(2,1)S(1)}, bf16[256,1024]{0,1:T(8,128)(2,1)S(1)}, u32[]{:S(2)}, u32[]{:S(2)}) collective-permute-start(bf16[256,1024]{0,1:T(8,128)(2,1)S(1)} %get-tuple-element.116), channel_id=1, source_target_pairs={{0,3},{1,0},{2,1},{3,2},{4,7},{5,4},{6,5},{7,6},{8,11},{9,8},{10,9... | collective-permute-start | bytes 1572872 | tf_op jit(solution)/shard_map/ppermute | solution.py:91
  243.1 70.8 %collective-permute-start.25 = (bf16[256,1024]{0,1:T(8,128)(2,1)S(1)}, bf16[256,1024]{0,1:T(8,128)(2,1)S(1)}, u32[]{:S(2)}, u32[]{:S(2)}) collective-permute-start(bf16[256,1024]{0,1:T(8,128)(2,1)S(1)} %get-tuple-element.117), channel_id=1, source_target_pairs={{0,2},{1,3},{2,0},{3,1},{4,6},{5,7},{6,4},{7,5},{8,10},{9,11},{10,... | collective-permute-start | bytes 1572872 | tf_op jit(solution)/shard_map/ppermute | solution.py:91
  244.9 69.1 %collective-permute-start.24 = (bf16[256,1024]{0,1:T(8,128)(2,1)S(1)}, bf16[256,1024]{0,1:T(8,128)(2,1)S(1)}, u32[]{:S(2)}, u32[]{:S(2)}) collective-permute-start(bf16[256,1024]{0,1:T(8,128)(2,1)S(1)} %get-tuple-element.115), channel_id=1, source_target_pairs={{0,1},{1,2},{2,3},{3,0},{4,5},{5,6},{6,7},{7,4},{8,9},{9,10},{10,1... | collective-permute-start | bytes 1572872 | tf_op jit(solution)/shard_map/ppermute | solution.py:91
  248.9 66.3 %collective-permute-start.20 = (bf16[256,1024]{0,1:T(8,128)(2,1)S(1)}, bf16[256,1024]{0,1:T(8,128)(2,1)S(1)}, u32[]{:S(2)}, u32[]{:S(2)}) collective-permute-start(bf16[256,1024]{0,1:T(8,128)(2,1)S(1)} %get-tuple-element.119), channel_id=1, source_target_pairs={{0,3},{1,0},{2,1},{3,2},{4,7},{5,4},{6,5},{7,6},{8,11},{9,8},{10,9... | collective-permute-start | bytes 1572872 | tf_op jit(solution)/shard_map/ppermute | solution.py:91
  252.8 81.6 %collective-permute-start.19 = (bf16[256,1024]{0,1:T(8,128)(2,1)S(1)}, bf16[256,1024]{0,1:T(8,128)(2,1)S(1)}, u32[]{:S(2)}, u32[]{:S(2)}) collective-permute-start(bf16[256,1024]{0,1:T(8,128)(2,1)S(1)} %get-tuple-element.120), channel_id=1, source_target_pairs={{0,2},{1,3},{2,0},{3,1},{4,6},{5,7},{6,4},{7,5},{8,10},{9,11},{10,... | collective-permute-start | bytes 1572872 | tf_op jit(solution)/shard_map/ppermute | solution.py:91
  263.6 70.8 %collective-permute-start.18 = (bf16[256,1024]{0,1:T(8,128)(2,1)S(1)}, bf16[256,1024]{0,1:T(8,128)(2,1)S(1)}, u32[]{:S(2)}, u32[]{:S(2)}) collective-permute-start(bf16[256,1024]{0,1:T(8,128)(2,1)S(1)} %get-tuple-element.118), channel_id=1, source_target_pairs={{0,1},{1,2},{2,3},{3,0},{4,5},{5,6},{6,7},{7,4},{8,9},{9,10},{10,1... | collective-permute-start | bytes 1572872 | tf_op jit(solution)/shard_map/ppermute | solution.py:91
  313.9 27.4 %collective-permute-start.39 = (bf16[512,1024]{1,0:T(8,128)(2,1)}, bf16[512,1024]{1,0:T(8,128)(2,1)}, u32[]{:S(2)}, u32[]{:S(2)}) collective-permute-start(bf16[512,1024]{1,0:T(8,128)(2,1)} %slice.596), channel_id=1, source_target_pairs={{0,4},{4,0},{8,12},{12,8},{1,5},{5,1},{9,13},{13,9},{2,6},{6,2},{1... | collective-permute-start | bytes 3145736 | tf_op jit(solution)/shard_map/ppermute | solution.py:32
  313.9 32.1 %collective-permute-start.42 = (bf16[512,1024]{1,0:T(8,128)(2,1)}, bf16[512,1024]{1,0:T(8,128)(2,1)}, u32[]{:S(2)}, u32[]{:S(2)}) collective-permute-start(bf16[512,1024]{1,0:T(8,128)(2,1)} %slice.595), channel_id=1, source_target_pairs={{0,4},{4,0},{8,12},{12,8},{1,5},{5,1},{9,13},{13,9},{2,6},{6,2},{1... | collective-permute-start | bytes 3145736 | tf_op jit(solution)/shard_map/ppermute | solution.py:32
  336.2 36.5 %collective-permute-start.28 = (bf16[256,1024]{0,1:T(8,128)(2,1)S(1)}, bf16[256,1024]{0,1:T(8,128)(2,1)}, u32[]{:S(2)}, u32[]{:S(2)}) collective-permute-start(bf16[256,1024]{0,1:T(8,128)(2,1)S(1)} %fusion.30), channel_id=1, source_target_pairs={{0,2},{1,3},{2,0},{3,1},{4,6},{5,7},{6,4},{7,5},{8,10},{9,11},{10,... | collective-permute-start | bytes 1572872 | tf_op jit(solution)/shard_map/ppermute | solution.py:81
  336.6 36.2 %collective-permute-start.27 = (bf16[256,1024]{0,1:T(8,128)(2,1)S(1)}, bf16[256,1024]{0,1:T(8,128)(2,1)}, u32[]{:S(2)}, u32[]{:S(2)}) collective-permute-start(bf16[256,1024]{0,1:T(8,128)(2,1)S(1)} %fusion.30), channel_id=1, source_target_pairs={{0,3},{1,0},{2,1},{3,2},{4,7},{5,4},{6,5},{7,6},{8,11},{9,8},{10,9... | collective-permute-start | bytes 1572872 | tf_op jit(solution)/shard_map/ppermute | solution.py:81
  344.5 72.0 %collective-permute-start.40 = (bf16[256,1024]{1,0:T(8,128)(2,1)}, bf16[256,1024]{1,0:T(8,128)(2,1)}, u32[]{:S(2)}, u32[]{:S(2)}) collective-permute-start(bf16[256,1024]{1,0:T(8,128)(2,1)} %slice.599), channel_id=1, source_target_pairs={{0,8},{4,12},{8,0},{12,4},{1,9},{5,13},{9,1},{13,5},{2,10},{6,14},... | collective-permute-start | bytes 1572872 | tf_op jit(solution)/shard_map/ppermute | solution.py:32
  348.7 69.2 %collective-permute-start.43 = (bf16[256,1024]{1,0:T(8,128)(2,1)}, bf16[256,1024]{1,0:T(8,128)(2,1)}, u32[]{:S(2)}, u32[]{:S(2)}) collective-permute-start(bf16[256,1024]{1,0:T(8,128)(2,1)} %slice.598), channel_id=1, source_target_pairs={{0,8},{4,12},{8,0},{12,4},{1,9},{5,13},{9,1},{13,5},{2,10},{6,14},... | collective-permute-start | bytes 1572872 | tf_op jit(solution)/shard_map/ppermute | solution.py:32
  390.1 31.3 %collective-permute-start.32 = (bf16[256,1024]{0,1:T(8,128)(2,1)}, bf16[256,1024]{0,1:T(8,128)(2,1)}, u32[]{:S(2)}, u32[]{:S(2)}) collective-permute-start(bf16[256,1024]{0,1:T(8,128)(2,1)} %get-tuple-element.113), channel_id=1, source_target_pairs={{0,3},{1,0},{2,1},{3,2},{4,7},{5,4},{6,5},{7,6},{8,11},{9,8},{10,9... | collective-permute-start | bytes 1572872 | tf_op jit(solution)/shard_map/ppermute | solution.py:91
  402.4 44.9 %collective-permute-start.31 = (bf16[256,1024]{0,1:T(8,128)(2,1)}, bf16[256,1024]{0,1:T(8,128)(2,1)}, u32[]{:S(2)}, u32[]{:S(2)}) collective-permute-start(bf16[256,1024]{0,1:T(8,128)(2,1)} %get-tuple-element.114), channel_id=1, source_target_pairs={{0,2},{1,3},{2,0},{3,1},{4,6},{5,7},{6,4},{7,5},{8,10},{9,11},{10,... | collective-permute-start | bytes 1572872 | tf_op jit(solution)/shard_map/ppermute | solution.py:91
  415.7 33.1 %collective-permute-start.30 = (bf16[256,1024]{0,1:T(8,128)(2,1)}, bf16[256,1024]{0,1:T(8,128)(2,1)S(1)}, u32[]{:S(2)}, u32[]{:S(2)}) collective-permute-start(bf16[256,1024]{0,1:T(8,128)(2,1)} %get-tuple-element.112), channel_id=1, source_target_pairs={{0,1},{1,2},{2,3},{3,0},{4,5},{5,6},{6,7},{7,4},{8,9},{9,10},{10,1... | collective-permute-start | bytes 1572872 | tf_op jit(solution)/shard_map/ppermute | solution.py:91
  416.5 76.1 %collective-permute-start.33 = (bf16[512,768]{1,0:T(8,128)(2,1)}, bf16[512,768]{1,0:T(8,128)(2,1)}, u32[]{:S(2)}, u32[]{:S(2)}) collective-permute-start(bf16[512,768]{1,0:T(8,128)(2,1)} %slice.597), channel_id=1, source_target_pairs={{0,4},{4,0},{8,12},{12,8},{1,5},{5,1},{9,13},{13,9},{2,6},{6,2},{1... | collective-permute-start | bytes 2359304 | tf_op jit(solution)/shard_map/ppermute | solution.py:32
  417.9 74.7 %collective-permute-start.38 = (bf16[256,256]{1,0:T(8,128)(2,1)S(1)}, bf16[256,256]{1,0:T(8,128)(2,1)S(1)}, u32[]{:S(2)}, u32[]{:S(2)}) collective-permute-start(bf16[256,256]{1,0:T(8,128)(2,1)S(1)} %fusion.31), channel_id=1, source_target_pairs={{0,16},{16,0},{1,17},{17,1},{2,18},{18,2},{3,19},{19,3},{4,20},{20... | collective-permute-start | bytes 393224 | tf_op jit(solution)/shard_map/ppermute | solution.py:32
  421.4 88.5 %collective-permute-start.41 = (bf16[256,1024]{1,0:T(8,128)(2,1)S(1)}, bf16[256,1024]{1,0:T(8,128)(2,1)}, u32[]{:S(2)}, u32[]{:S(2)}) collective-permute-start(bf16[256,1024]{1,0:T(8,128)(2,1)S(1)} %fusion.22), channel_id=1, source_target_pairs={{0,16},{16,0},{1,17},{17,1},{2,18},{18,2},{3,19},{19,3},{4,20},{20... | collective-permute-start | bytes 1572872 | tf_op jit(solution)/shard_map/ppermute | solution.py:32
  447.3 59.9 %collective-permute-start.44 = (bf16[256,1024]{1,0:T(8,128)(2,1)}, bf16[256,1024]{1,0:T(8,128)(2,1)}, u32[]{:S(2)}, u32[]{:S(2)}) collective-permute-start(bf16[256,1024]{1,0:T(8,128)(2,1)} %fusion.21), channel_id=1, source_target_pairs={{0,16},{16,0},{1,17},{17,1},{2,18},{18,2},{3,19},{19,3},{4,20},{20... | collective-permute-start | bytes 1572872 | tf_op jit(solution)/shard_map/ppermute | solution.py:32
  (53 other events, 1317.7 us)

commit v2 on v1

--- a/solution.py
+++ b/solution.py
@@ -75,23 +75,11 @@
 
 
 def gather_rows(own):
-    size = lax.axis_size("head")
-    pieces = [own]
-    for step in range(1, size):
-        pieces.append(lax.ppermute(own, "head", [(at, (at - step) % size) for at in range(size)]))
-    return jnp.concatenate(pieces, axis=0)
+    return lax.all_gather(own, "head", axis=0, tiled=True)
 
 
 def scatter_rows(total):
-    size = lax.axis_size("head")
-    rows = total.shape[0] // size
-    out = total[:rows].astype(F32)
-    for step in range(1, size):
-        piece = total[step * rows : (step + 1) * rows]
-        out = out + lax.ppermute(
-            piece, "head", [(at, (at + step) % size) for at in range(size)]
-        ).astype(F32)
-    return out
+    return lax.psum_scatter(total, "head", scatter_dimension=0, tiled=True).astype(F32)
 
 
 def scatter_grad(grad):
@@ -104,6 +92,22 @@
     if lax.axis_size("rep") == 2:
         return own.astype(F32) + swap(own, "rep", 1).astype(F32)
     return lax.psum(own.astype(F32), "rep")
+
+
+def scatter_small(blocks):
+    near = blocks[:2] + swap(blocks[2:], "shard", 1)
+    own = near[:1] + swap(near[1:], "shard", 2)
+    if lax.axis_size("rep") == 2:
+        return own + swap(own, "rep", 1)
+    return lax.psum(own, "rep")
+
+
+def head_sum(value):
+    bit = 1
+    while bit < lax.axis_size("head"):
+        value = value + swap(value, "head", bit)
+        bit *= 2
+    return value
 
 
 def forward_kernel(count, block, slopes, starts, q_ref, k_ref, v_ref, o_ref, lse_ref):
@@ -299,7 +303,7 @@
     qkv = ((jnp.dot(normed_one, qkv_w, preferred_element_type=F32) + qkv_b) * factor).astype(BF)
     position = place * heads_here + jnp.arange(heads_here, dtype=jnp.int32) + 1
     slopes = jnp.exp2(-8.0 * position.astype(F32) / HEADS)
-    starts = lax.rem(jnp.arange(group, dtype=jnp.int32) - place + group, group) * block
+    starts = jnp.arange(group, dtype=jnp.int32) * block
     mixed, logsum = attend(qkv, slopes, starts, block)
     resid = inputs + scatter_rows(contract(mixed, out_w, 1, 1).astype(BF)) + out_b
     normed_two = gather_rows(layer_norm(resid, gain_two, shift_two).astype(BF))
@@ -334,42 +338,54 @@
     input_part, gain_one_grad, shift_one_grad = first_back(first_grad)
     input_grad = blocks_back((resid_grad + input_part).astype(BF), shard, 1)
 
-    stats = jnp.stack(
-        [gain_one_grad, shift_one_grad, out_b_grad, gain_two_grad, shift_two_grad, down_b_grad]
-    )
-    stats = blocks_back(stats, shard, 1).reshape(-1)
-    biases = jnp.concatenate([query_b_grad, value_b_grad, up_b_grad])
-    mine = (jnp.arange(group, dtype=jnp.int32) == place)[:, None]
-    biases = jnp.where(mine, biases[None, :], 0.0).reshape(-1)
-    sums = lax.psum(jnp.concatenate([stats, biases]), ("rep", "shard", "head"))
-    stats = sums[: stats.size].reshape(6, 4, feats)
-    stats = lax.dynamic_index_in_dim(stats, shard, 1, keepdims=False)
-    biases = lax.dynamic_index_in_dim(
-        sums[6 * 4 * feats :].reshape(group, -1), place, 0, keepdims=False
-    )
-
-    def own_part(values, rows):
-        parts = values.reshape(rows, 4, -1)
-        return lax.dynamic_index_in_dim(parts, shard, 1, keepdims=False)
+    def feature_blocks(values):
+        return values.reshape(-1, 4, feats).transpose(1, 0, 2).reshape(4, -1)
+
+    def bias_blocks(values, rows):
+        parts = values.reshape(rows, 4, -1).transpose(1, 0, 2).reshape(4, -1)
+        return blocks_by_xor(parts, shard, 0)
+
+    late = scatter_small(
+        jnp.concatenate(
+            [
+                feature_blocks(jnp.stack([gain_one_grad, shift_one_grad])),
+                bias_blocks(jnp.stack([query_b_grad, value_b_grad]), 2 * heads_here),
+            ],
+            axis=1,
+        )
+    )
+    late_stats = head_sum(late[:, : 2 * feats]).reshape(2, feats)
+    late_bias = late[:, 2 * feats :].reshape(2, heads_here, -1)
+    early = scatter_small(
+        jnp.concatenate(
+            [
+                feature_blocks(jnp.stack([out_b_grad, gain_two_grad, shift_two_grad, down_b_grad])),
+                bias_blocks(up_b_grad, b_up.shape[0]),
+            ],
+            axis=1,
+        )
+    )
+    early_stats = head_sum(early[:, : 4 * feats]).reshape(4, feats)
+    early_bias = early[:, 4 * feats :].reshape(b_up.shape[0], -1)
 
     return (
         output,
         input_grad,
-        stats[0],
-        stats[1],
+        late_stats[0],
+        late_stats[1],
         qkv_w_grad[:, :width],
         qkv_w_grad[:, width : 2 * width],
         qkv_w_grad[:, 2 * width :],
-        own_part(biases[:width], heads_here),
-        own_part(biases[width : 2 * width], heads_here),
+        late_bias[0],
+        late_bias[1],
         out_w_grad.T,
-        stats[2],
-        stats[3],
-        stats[4],
+        early_stats[0],
+        early_stats[1],
+        early_stats[2],
         up_w_grad,
-        own_part(biases[2 * width :], b_up.shape[0]),
+        early_bias,
         down_w_grad.T,
-        stats[5],
+        early_stats[3],
     )
 
 

time: 525 us -> 476 us (0.907)
  starting transfers between devices: 121 us -> 25.1 us
  waiting for transfers between devices: 206 us -> 273 us
  blocking collectives: 46.7 us -> 6.22 us
  matrix products: 38.4 us -> 51.8 us
  between operations: 2.21 us -> 15.5 us
  local copies, waits for them, and re-layouts: 49.7 us -> 38 us
  other arithmetic: 31.5 us -> 37.9 us
    ppermute x24 -> x0, waiting for transfers between devices: 199 us -> none  [the longest x12 113 us: scatter_rows(): lax.ppermute(piece, 'head', [(at, (at + step) % size) for at in range(siz...]
    reduce_scatter x0 -> x4, waiting for transfers between devices: none -> 106 us  [scatter_rows(): lax.psum_scatter(total, 'head', scatter_dimension=0, tiled=True).astype(F32)]
    ppermute x24 -> x0, starting transfers between devices: 104 us -> none  [the longest x12 60.2 us: scatter_rows(): lax.ppermute(piece, 'head', [(at, (at + step) % size) for at in range(siz...]
    all_gather x0 -> x4, waiting for transfers between devices: none -> 89.1 us  [gather_rows(): return lax.all_gather(own, 'head', axis=0, tiled=True)]
    ppermute x21 -> x31, waiting for transfers between devices: 8 us -> 77.8 us  [swap(): return lax.ppermute(value, axis, [(at, at ^ bit) for at in range(size)])]
    psum x1 -> x0, blocking collectives: 39.9 us -> none  [body(): sums = lax.psum(jnp.concatenate([stats, biases]), ('rep', 'shard', 'head'))]
    dot_general x8, matrix products: 22 us -> 31.4 us  [contract(): lax.dot_general(left, right, (((left_dim,), (right_dim,)), ((), ())), pre...]
    unnamed x102 -> x84, local copies, waits for them, and re-layouts: 25.5 us -> 19 us
  transfers between devices with their start and end apart: 45 -> 39, of which waited for: 15 -> 23; matrix products, arithmetic and copies ran while one was open for 19% -> 17% of each run, Pallas kernels for 4% -> 3%
where the time goes in v2:
time: 476 us; the launch traced here: 468 us
  waiting for transfers between devices  273 us (57%)
  matrix products  51.8 us (11%)
  local copies, waits for them, and re-layouts  38 us (8%)
  other arithmetic  37.9 us (8%)
  starting transfers between devices  25.1 us (5%)
  Pallas kernels  20 us (4%)
  between operations  15.5 us (3%)
  blocking collectives  6.22 us (1%)
    reduce_scatter x4, waiting for transfers between devices, scatter_rows(): lax.psum_scatter(total, 'head', scatter_dimension=0, tiled=True).astype(F32)  106 us
    all_gather x4, waiting for transfers between devices, gather_rows(): return lax.all_gather(own, 'head', axis=0, tiled=True)  89.1 us
    ppermute x31, waiting for transfers between devices, swap(): return lax.ppermute(value, axis, [(at, at ^ bit) for at in range(size)])  77.8 us
    dot_general x8, matrix products, contract(): lax.dot_general(left, right, (((left_dim,), (right_dim,)), ((), ())), pre...  31.4 us
    ppermute x31, starting transfers between devices, swap(): return lax.ppermute(value, axis, [(at, at ^ bit) for at in range(size)])  24.1 us
    unnamed x84, local copies, waits for them, and re-layouts  19 us
    pallas_call x1, Pallas kernels, attend_back(): pl.pallas_call(partial(backward_kernel, count, block), grid=(pairs,), in_...  12.1 us
  transfers between devices with their start and end apart: 39, of which 23 were waited for; matrix products, arithmetic and copies ran while one was open for 17% of the time, Pallas kernels for 3%

profile of v2, /device:TPU:0, one launch (start us, length us, event | category | flops | bytes accessed | tf_op | source)
XLA Modules:
  0.0 467.8 jit_solution(9562381208881263282)
XLA Ops:
  9.5 4.1 concatenate.59
  13.6 6.2 %all-gather.1 = bf16[4,1,1920]{2,1,0:T(2,128)(2,1)S(1)} all-gather(bf16[1,1,1920]{2,1,0:T(2,128)(2,1)S(1)} %reshape.510), channel_id=2, replica_groups=mesh['rep'=2,'shard'=4,'head'=4] {'shard'}, dimensions={0}, use_global_device_ids=true | all-gather | bytes 19200 | tf_op jit(solution)/shard_map/all_gather | solution.py:280
  25.3 12.4 %collective-permute-done = bf16[256,1024]{0,1:T(8,128)(2,1)S(1)} collective-permute-done((bf16[256,1024]{0,1:T(8,128)(2,1)S(1)}, bf16[256,1024]{0,1:T(8,128)(2,1)S(1)}, u32[]{:S(2)}, u32[]{:S(2)}) %collective-permute-start) | collective-permute-done | bytes 524320 | tf_op jit(solution)/shard_map/ppermute | solution.py:32
  39.6 4.5 pad_maximum_fusion
  44.1 26.4 %all-gather.7.cloned.1.call-done = bf16[1024,1024]{1,0:T(8,128)(2,1)} async-done(((bf16[256,1024]{1,0:T(8,128)(2,1)}), bf16[1024,1024]{1,0:T(8,128)(2,1)}) %all-gather.7.cloned.1.call-update) | async-done | bytes 2097168 | tf_op jit(solution)/shard_map/all_gather | solution.py:78
  70.5 3.9 multiply_convert_fusion.1.q_ref.k_ref.v_ref
  74.4 7.9 %attend.1 = (bf16[1024,256]{1,0:T(8,128)(2,1)S(1)}, f32[2,8,256]{2,1,0:T(8,128)S(1)}) custom-call(f32[4]{0:T(128)S(1)} %multiply_exponential_fusion.slopes, s32[4]{0:T(128)S(1)} %iota_multiply_fusion.starts, bf16[1024,768]{1,0:T(8,128)(2,1)S(1)} %multiply_convert_fusion.1.q_ref.k_ref.v_ref, bf16[1024,768]{1,0:T(8,128)(2,1)S(1)} %multiply_convert_fusion.1.q_ref.k_ref.v_ref, ...), custom_call_target="tpu_custom_call" | custom-call | tf_op jit(solution)/shard_map/attend/pallas_call | solution.py:209
  84.5 42.7 %reduce-scatter.5.cloned.1.call-done = bf16[256,1024]{1,0:T(8,128)(2,1)} async-done(((bf16[1024,1024]{1,0:T(8,128)(2,1)}), bf16[256,1024]{1,0:T(8,128)(2,1)}) %reduce-scatter.5.cloned.1.call-update) | async-done | bytes 524304 | tf_op jit(solution)/shard_map/reduce_scatter | solution.py:82
  136.0 12.6 %collective-permute-done.3 = bf16[256,1024]{1,0:T(8,128)(2,1)} collective-permute-done((bf16[256,1024]{1,0:T(8,128)(2,1)}, bf16[256,1024]{1,0:T(8,128)(2,1)}, u32[]{:S(2)}, u32[]{:S(2)}) %collective-permute-start.3) | collective-permute-done | bytes 524320 | tf_op jit(solution)/shard_map/ppermute | solution.py:32
  150.7 7.8 %collective-permute-done.6 = bf16[256,1024]{0,1:T(8,128)(2,1)} collective-permute-done((bf16[256,1024]{0,1:T(8,128)(2,1)}, bf16[256,1024]{0,1:T(8,128)(2,1)}, u32[]{:S(2)}, u32[]{:S(2)}) %collective-permute-start.6) | collective-permute-done | bytes 524320 | tf_op jit(solution)/shard_map/ppermute | solution.py:32
  164.1 12.3 %all-gather.9.cloned.1.call-done = bf16[1024,1024]{1,0:T(8,128)(2,1)} async-done(((bf16[256,1024]{1,0:T(8,128)(2,1)}), bf16[1024,1024]{1,0:T(8,128)(2,1)}) %all-gather.9.cloned.1.call-update) | async-done | bytes 2097168 | tf_op jit(solution)/shard_map/all_gather | solution.py:78
  176.4 6.5 %fusion.52 = f32[1024,1024]{1,0:T(8,128)} fusion(bf16[1024,1024]{1,0:T(8,128)(2,1)} %all-gather.9.cloned.1.call-done, bf16[1024,1024]{1,0:T(8,128)(2,1)} %constant_dynamic-update-slice_fusion), kind=kOutput, calls=%fused_computation.211 | convolution fusion | flops 2147483648 | bytes 8388608 | tf_op jit(solution)/shard_map/dot_general | solution.py:310
  183.0 40.2 %all-gather.11.cloned.1.call-done = bf16[1024,1024]{1,0:T(8,128)(2,1)} async-done(((bf16[256,1024]{1,0:T(8,128)(2,1)}), bf16[1024,1024]{1,0:T(8,128)(2,1)}) %all-gather.11.cloned.1.call-update) | async-done | bytes 2097168 | tf_op jit(solution)/shard_map/all_gather | solution.py:78
  223.2 7.7 %convert_reduce_fusion = (f32[1024]{0:T(1024)S(1)}, bf16[1024,1024]{1,0:T(8,128)(2,1)S(1)}) fusion(f32[1024,1024]{1,0:T(8,128)} %fusion.52, f32[1024]{0:T(1024)S(1)} %reshape.506, bf16[1024,1024]{1,0:T(8,128)(2,1)} %all-gather.11.cloned.1.call-done, bf16[256,1024]{0,1:T(8,128)(2,1)} %collective-permute-done.8, bf16[256,1024]{0,1:T(8,128)(2,1)} %collective-permute-done.7, ...), kind=kOutput, calls=%fused_computation.9 | convolution fusion | flops 2179988480 | bytes 10493952 | tf_op jit(solution)/shard_map/dot_general | solution.py:312
  232.3 5.3 %convolution_convert_fusion = bf16[1024,1024]{1,0:T(8,128)(2,1)} fusion(bf16[1024,1024]{1,0:T(8,128)(2,1)S(1)} %get-tuple-element.154, bf16[1024,1024]{1,0:T(8,128)(2,1)} %constant_dynamic-update-slice_fusion), kind=kOutput, calls=%fused_computation.18 | convolution fusion | flops 2148532224 | bytes 6291456 | tf_op jit(solution)/shard_map/dot_general | solution.py:18
  237.6 6.9 %convolution_convert_fusion.1 = bf16[1024,1024]{1,0:T(8,128)(2,1)} fusion(bf16[256,1024]{0,1:T(8,128)(2,1)} %collective-permute-done.8, bf16[256,1024]{0,1:T(8,128)(2,1)} %collective-permute-done.7, bf16[256,1024]{0,1:T(8,128)(2,1)} %collective-permute-done.6, bf16[256,1024]{0,1:T(8,128)(2,1)} %bitcast.117, f32[1024,1024]{1,0:T(8,128)} %fusion.52, ...), kind=kOutput, calls=%fused_computation.19 | convolution fusion | flops 2167406592 | bytes 8392704 | tf_op jit(solution)/shard_map/dot_general | solution.py:18
  244.8 6.7 %fusion.55 = f32[1024,1024]{1,0:T(8,128)} fusion(bf16[1024,1024]{1,0:T(8,128)(2,1)} %all-gather.9.cloned.1.call-done, bf16[1024,1024]{1,0:T(8,128)(2,1)} %copy-done.34), kind=kOutput, calls=%fused_computation.214 | convolution fusion | flops 2147483648 | bytes 8388608 | tf_op jit(solution)/shard_map/dot_general | solution.py:18
  251.5 2.9 slice.698
  254.4 2.6 fusion.46
  260.6 19.7 %reduce-scatter.9.cloned.1.call-done = bf16[256,1024]{1,0:T(8,128)(2,1)} async-done(((bf16[1024,1024]{1,0:T(8,128)(2,1)}), bf16[256,1024]{1,0:T(8,128)(2,1)}) %reduce-scatter.9.cloned.1.call-update) | async-done | bytes 524304 | tf_op jit(solution)/shard_map/reduce_scatter | solution.py:82
  281.8 43.9 %reduce-scatter.7.cloned.1.call-done = bf16[256,1024]{1,0:T(8,128)(2,1)} async-done(((bf16[1024,1024]{1,0:T(8,128)(2,1)}), bf16[256,1024]{1,0:T(8,128)(2,1)}) %reduce-scatter.7.cloned.1.call-update) | async-done | bytes 524304 | tf_op jit(solution)/shard_map/reduce_scatter | solution.py:82
  325.7 2.8 fusion.23
  341.5 8.6 %collective-permute-done.26 = bf16[256,1024]{1,0:T(8,128)(2,1)} collective-permute-done((bf16[256,1024]{1,0:T(8,128)(2,1)S(1)}, bf16[256,1024]{1,0:T(8,128)(2,1)}, u32[]{:S(2)}, u32[]{:S(2)}) %collective-permute-start.26) | collective-permute-done | bytes 524320 | tf_op jit(solution)/shard_map/ppermute | solution.py:32
  353.1 6.8 %collective-permute-done.29 = bf16[256,1024]{1,0:T(8,128)(2,1)} collective-permute-done((bf16[256,1024]{1,0:T(8,128)(2,1)}, bf16[256,1024]{1,0:T(8,128)(2,1)}, u32[]{:S(2)}, u32[]{:S(2)}) %collective-permute-start.29) | collective-permute-done | bytes 524320 | tf_op jit(solution)/shard_map/ppermute | solution.py:32
  366.3 10.1 %all-gather.13.cloned.1.call-done = bf16[1024,1024]{1,0:T(8,128)(2,1)} async-done(((bf16[256,1024]{1,0:T(8,128)(2,1)}), bf16[1024,1024]{1,0:T(8,128)(2,1)}) %all-gather.13.cloned.1.call-update) | async-done | bytes 2097168 | tf_op jit(solution)/shard_map/all_gather | solution.py:78
  378.7 12.1 %attend_back.1 = (bf16[1024,256]{1,0:T(8,128)(2,1)S(1)}, bf16[1024,256]{1,0:T(8,128)(2,1)S(1)}, bf16[1024,256]{1,0:T(8,128)(2,1)S(1)}) custom-call(f32[4]{0:T(128)S(1)} %multiply_exponential_fusion.slopes, s32[4]{0:T(128)S(1)} %iota_multiply_fusion.starts, bf16[1024,768]{1,0:T(8,128)(2,1)S(1)} %multiply_convert_fusion.1.q_ref.k_ref.v_ref, ...), custom_call_target="tpu_custom_call" | custom-call | tf_op jit(solution)/shard_map/attend_back/pallas_call | solution.py:232
  393.0 3.1 convolution_convert_fusion.3
  401.4 2.8 collective-permute-done.23
  405.3 3.9 fusion.53
  421.4 7.5 %collective-permute-done.15 = bf16[256,768]{1,0:T(8,128)(2,1)S(1)} collective-permute-done((bf16[256,768]{1,0:T(8,128)(2,1)S(1)}, bf16[256,768]{1,0:T(8,128)(2,1)S(1)}, u32[]{:S(2)}, u32[]{:S(2)}) %collective-permute-start.15) | collective-permute-done | bytes 393248 | tf_op jit(solution)/shard_map/ppermute | solution.py:32
  431.3 7.7 %collective-permute-done.16 = bf16[256,768]{1,0:T(8,128)(2,1)S(1)} collective-permute-done((bf16[256,768]{1,0:T(8,128)(2,1)S(1)}, bf16[256,768]{1,0:T(8,128)(2,1)S(1)}, u32[]{:S(2)}, u32[]{:S(2)}) %collective-permute-start.16) | collective-permute-done | bytes 393248 | tf_op jit(solution)/shard_map/ppermute | solution.py:32
  449.2 2.6 collective-permute-done.11
  (271 shorter events, 101.1 us)
Async XLA Ops:
  7.2 63.3 %all-gather.7.cloned.1.call-start = ((), (), s32[]{:S(2)}) async-start(), calls=%async_computation.4 | async-start | bytes 2621440 | tf_op jit(solution)/shard_map/all_gather | solution.py:78
  22.8 104.4 %reduce-scatter.5.cloned.1.call-start = ((), (), s32[]{:S(2)}) async-start(), calls=%async_computation.5 | async-start | bytes 2621440 | tf_op jit(solution)/shard_map/reduce_scatter | solution.py:82
  23.2 14.4 %collective-permute-start = (bf16[256,1024]{0,1:T(8,128)(2,1)S(1)}, bf16[256,1024]{0,1:T(8,128)(2,1)S(1)}, u32[]{:S(2)}, u32[]{:S(2)}) collective-permute-start(bf16[256,1024]{0,1:T(8,128)(2,1)S(1)} %pad_maximum_fusion.4), channel_id=1, source_target_pairs={{0,8},{4,12},{8,0},{12,4},{1,9},{5,13},{9,1},{13,5},{2,10},{6,14},... | collective-permute-start | bytes 1572872 | tf_op jit(solution)/shard_map/ppermute | solution.py:32
  25.2 12.9 %collective-permute-start.1 = (bf16[256,1024]{0,1:T(8,128)(2,1)S(1)}, bf16[256,1024]{0,1:T(8,128)(2,1)S(1)}, u32[]{:S(2)}, u32[]{:S(2)}) collective-permute-start(bf16[256,1024]{0,1:T(8,128)(2,1)S(1)} %pad_maximum_fusion.4), channel_id=1, source_target_pairs={{0,4},{4,0},{8,12},{12,8},{1,5},{5,1},{9,13},{13,9},{2,6},{6,2},{1... | collective-permute-start | bytes 1572872 | tf_op jit(solution)/shard_map/ppermute | solution.py:32
  84.4 92.1 %all-gather.9.cloned.1.call-start = ((), (), s32[]{:S(2)}) async-start(), calls=%async_computation.6 | async-start | bytes 2621440 | tf_op jit(solution)/shard_map/all_gather | solution.py:78
  131.0 92.2 %all-gather.11.cloned.1.call-start = ((), (), s32[]{:S(2)}) async-start(), calls=%async_computation.8 | async-start | bytes 2621440 | tf_op jit(solution)/shard_map/all_gather | solution.py:78
  133.2 147.2 %reduce-scatter.9.cloned.1.call-start = ((), (), s32[]{:S(2)}) async-start(), calls=%async_computation.9 | async-start | bytes 2621440 | tf_op jit(solution)/shard_map/reduce_scatter | solution.py:82
  133.4 15.2 %collective-permute-start.3 = (bf16[256,1024]{1,0:T(8,128)(2,1)}, bf16[256,1024]{1,0:T(8,128)(2,1)}, u32[]{:S(2)}, u32[]{:S(2)}) collective-permute-start(bf16[256,1024]{1,0:T(8,128)(2,1)} %param.29), channel_id=1, source_target_pairs={{0,8},{4,12},{8,0},{12,4},{1,9},{5,13},{9,1},{13,5},{2,10},{6,14},... | collective-permute-start | bytes 1572872 | tf_op jit(solution)/shard_map/ppermute | solution.py:32
  134.9 23.6 %collective-permute-start.6 = (bf16[256,1024]{0,1:T(8,128)(2,1)}, bf16[256,1024]{0,1:T(8,128)(2,1)}, u32[]{:S(2)}, u32[]{:S(2)}) collective-permute-start(bf16[256,1024]{0,1:T(8,128)(2,1)} %bitcast.114), channel_id=1, source_target_pairs={{0,8},{4,12},{8,0},{12,4},{1,9},{5,13},{9,1},{13,5},{2,10},{6,14},... | collective-permute-start | bytes 1572872 | tf_op jit(solution)/shard_map/ppermute | solution.py:32
  135.5 24.9 %collective-permute-start.4 = (bf16[256,1024]{1,0:T(8,128)(2,1)}, bf16[256,1024]{1,0:T(8,128)(2,1)}, u32[]{:S(2)}, u32[]{:S(2)}) collective-permute-start(bf16[256,1024]{1,0:T(8,128)(2,1)} %param.29), channel_id=1, source_target_pairs={{0,4},{4,0},{8,12},{12,8},{1,5},{5,1},{9,13},{13,9},{2,6},{6,2},{1... | collective-permute-start | bytes 1572872 | tf_op jit(solution)/shard_map/ppermute | solution.py:32
  135.5 47.5 %collective-permute-start.7 = (bf16[256,1024]{0,1:T(8,128)(2,1)}, bf16[256,1024]{0,1:T(8,128)(2,1)}, u32[]{:S(2)}, u32[]{:S(2)}) collective-permute-start(bf16[256,1024]{0,1:T(8,128)(2,1)} %bitcast.115), channel_id=1, source_target_pairs={{0,4},{4,0},{8,12},{12,8},{1,5},{5,1},{9,13},{13,9},{2,6},{6,2},{1... | collective-permute-start | bytes 1572872 | tf_op jit(solution)/shard_map/ppermute | solution.py:32
  148.6 13.7 %collective-permute-start.5 = (bf16[256,1024]{1,0:T(8,128)(2,1)}, bf16[256,1024]{1,0:T(8,128)(2,1)}, u32[]{:S(2)}, u32[]{:S(2)}) collective-permute-start(bf16[256,1024]{1,0:T(8,128)(2,1)} %collective-permute-done.3), channel_id=1, source_target_pairs={{0,4},{4,0},{8,12},{12,8},{1,5},{5,1},{9,13},{13,9},{2,6},{6,2},{1... | collective-permute-start | bytes 1572872 | tf_op jit(solution)/shard_map/ppermute | solution.py:32
  158.5 24.5 %collective-permute-start.8 = (bf16[256,1024]{0,1:T(8,128)(2,1)}, bf16[256,1024]{0,1:T(8,128)(2,1)}, u32[]{:S(2)}, u32[]{:S(2)}) collective-permute-start(bf16[256,1024]{0,1:T(8,128)(2,1)} %collective-permute-done.6), channel_id=1, source_target_pairs={{0,4},{4,0},{8,12},{12,8},{1,5},{5,1},{9,13},{13,9},{2,6},{6,2},{1... | collective-permute-start | bytes 1572872 | tf_op jit(solution)/shard_map/ppermute | solution.py:32
  237.6 88.1 %reduce-scatter.7.cloned.1.call-start = ((), (), s32[]{:S(2)}) async-start(), calls=%async_computation.7 | async-start | bytes 2621440 | tf_op jit(solution)/shard_map/reduce_scatter | solution.py:82
  244.5 131.8 %all-gather.13.cloned.1.call-start = ((), (), s32[]{:S(2)}) async-start(), calls=%async_computation.10 | async-start | bytes 2621440 | tf_op jit(solution)/shard_map/all_gather | solution.py:78
  254.4 76.9 %collective-permute-start.25 = (bf16[512,1024]{1,0:T(8,128)(2,1)}, bf16[512,1024]{1,0:T(8,128)(2,1)}, u32[]{:S(2)}, u32[]{:S(2)}) collective-permute-start(bf16[512,1024]{1,0:T(8,128)(2,1)} %slice.698), channel_id=1, source_target_pairs={{0,4},{4,0},{8,12},{12,8},{1,5},{5,1},{9,13},{13,9},{2,6},{6,2},{1... | collective-permute-start | bytes 3145736 | tf_op jit(solution)/shard_map/ppermute | solution.py:32
  260.1 76.4 %collective-permute-start.28 = (bf16[512,1024]{1,0:T(8,128)(2,1)}, bf16[512,1024]{1,0:T(8,128)(2,1)}, u32[]{:S(2)}, u32[]{:S(2)}) collective-permute-start(bf16[512,1024]{1,0:T(8,128)(2,1)} %slice.697), channel_id=1, source_target_pairs={{0,4},{4,0},{8,12},{12,8},{1,5},{5,1},{9,13},{13,9},{2,6},{6,2},{1... | collective-permute-start | bytes 3145736 | tf_op jit(solution)/shard_map/ppermute | solution.py:32
  331.0 109.1 %reduce-scatter.11.cloned.1.call-start = ((), (), s32[]{:S(2)}) async-start(), calls=%async_computation.11 | async-start | bytes 2621440 | tf_op jit(solution)/shard_map/reduce_scatter | solution.py:82
  335.0 15.0 %collective-permute-start.26 = (bf16[256,1024]{1,0:T(8,128)(2,1)S(1)}, bf16[256,1024]{1,0:T(8,128)(2,1)}, u32[]{:S(2)}, u32[]{:S(2)}) collective-permute-start(bf16[256,1024]{1,0:T(8,128)(2,1)S(1)} %slice.701), channel_id=1, source_target_pairs={{0,8},{4,12},{8,0},{12,4},{1,9},{5,13},{9,1},{13,5},{2,10},{6,14},... | collective-permute-start | bytes 1572872 | tf_op jit(solution)/shard_map/ppermute | solution.py:32
  340.5 19.4 %collective-permute-start.29 = (bf16[256,1024]{1,0:T(8,128)(2,1)}, bf16[256,1024]{1,0:T(8,128)(2,1)}, u32[]{:S(2)}, u32[]{:S(2)}) collective-permute-start(bf16[256,1024]{1,0:T(8,128)(2,1)} %slice.700), channel_id=1, source_target_pairs={{0,8},{4,12},{8,0},{12,4},{1,9},{5,13},{9,1},{13,5},{2,10},{6,14},... | collective-permute-start | bytes 1572872 | tf_op jit(solution)/shard_map/ppermute | solution.py:32
  351.6 12.0 %collective-permute-start.27 = (bf16[256,1024]{1,0:T(8,128)(2,1)S(1)}, bf16[256,1024]{1,0:T(8,128)(2,1)S(1)}, u32[]{:S(2)}, u32[]{:S(2)}) collective-permute-start(bf16[256,1024]{1,0:T(8,128)(2,1)S(1)} %fusion.26), channel_id=1, source_target_pairs={{0,16},{16,0},{1,17},{17,1},{2,18},{18,2},{3,19},{19,3},{4,20},{20... | collective-permute-start | bytes 1572872 | tf_op jit(solution)/shard_map/ppermute | solution.py:32
  361.9 35.8 %collective-permute-start.30 = (bf16[256,1024]{1,0:T(8,128)(2,1)}, bf16[256,1024]{1,0:T(8,128)(2,1)}, u32[]{:S(2)}, u32[]{:S(2)}) collective-permute-start(bf16[256,1024]{1,0:T(8,128)(2,1)} %fusion.25), channel_id=1, source_target_pairs={{0,16},{16,0},{1,17},{17,1},{2,18},{18,2},{3,19},{19,3},{4,20},{20... | collective-permute-start | bytes 1572872 | tf_op jit(solution)/shard_map/ppermute | solution.py:32
  364.7 31.4 %collective-permute-start.21 = (f32[1,1280]{1,0:T(1,128)S(1)}, f32[1,1280]{1,0:T(1,128)S(1)}, u32[]{:S(2)}, u32[]{:S(2)}) collective-permute-start(f32[1,1280]{1,0:T(1,128)S(1)} %slice.363), channel_id=1, source_target_pairs={{0,8},{4,12},{8,0},{12,4},{1,9},{5,13},{9,1},{13,5},{2,10},{6,14},... | collective-permute-start | bytes 15368 | tf_op jit(solution)/shard_map/ppermute | solution.py:32
  396.2 4.2 collective-permute-start.22
  400.4 3.7 collective-permute-start.23
  404.1 8.4 %collective-permute-start.24 = (f32[1,1024]{1,0:T(1,128)S(1)}, f32[1,1024]{1,0:T(1,128)S(1)}, u32[]{:S(2)}, u32[]{:S(2)}) collective-permute-start(f32[1,1024]{1,0:T(1,128)S(1)} %slice_add_fusion.13), channel_id=1, source_target_pairs={{0,2},{1,3},{2,0},{3,1},{4,6},{5,7},{6,4},{7,5},{8,10},{9,11},{10,... | collective-permute-start | bytes 12296 | tf_op jit(solution)/shard_map/ppermute | solution.py:32
  409.3 7.0 %collective-permute-start.14 = (bf16[512,768]{1,0:T(8,128)(2,1)S(1)}, bf16[512,768]{1,0:T(8,128)(2,1)S(1)}, u32[]{:S(2)}, u32[]{:S(2)}) collective-permute-start(bf16[512,768]{1,0:T(8,128)(2,1)S(1)} %slice.699), channel_id=1, source_target_pairs={{0,4},{4,0},{8,12},{12,8},{1,5},{5,1},{9,13},{13,9},{2,6},{6,2},{1... | collective-permute-start | bytes 2359304 | tf_op jit(solution)/shard_map/ppermute | solution.py:32
  414.7 5.6 %collective-permute-start.18 = (bf16[256,256]{1,0:T(8,128)(2,1)S(1)}, bf16[256,256]{1,0:T(8,128)(2,1)S(1)}, u32[]{:S(2)}, u32[]{:S(2)}) collective-permute-start(bf16[256,256]{1,0:T(8,128)(2,1)S(1)} %slice.704), channel_id=1, source_target_pairs={{0,8},{4,12},{8,0},{12,4},{1,9},{5,13},{9,1},{13,5},{2,10},{6,14},... | collective-permute-start | bytes 393224 | tf_op jit(solution)/shard_map/ppermute | solution.py:32
  417.9 10.9 %collective-permute-start.15 = (bf16[256,768]{1,0:T(8,128)(2,1)S(1)}, bf16[256,768]{1,0:T(8,128)(2,1)S(1)}, u32[]{:S(2)}, u32[]{:S(2)}) collective-permute-start(bf16[256,768]{1,0:T(8,128)(2,1)S(1)} %slice.702), channel_id=1, source_target_pairs={{0,8},{4,12},{8,0},{12,4},{1,9},{5,13},{9,1},{13,5},{2,10},{6,14},... | collective-permute-start | bytes 1179656 | tf_op jit(solution)/shard_map/ppermute | solution.py:32
  420.4 10.1 %collective-permute-start.19 = (bf16[256,256]{1,0:T(8,128)(2,1)S(1)}, bf16[256,256]{1,0:T(8,128)(2,1)S(1)}, u32[]{:S(2)}, u32[]{:S(2)}) collective-permute-start(bf16[256,256]{1,0:T(8,128)(2,1)S(1)} %fusion.32), channel_id=1, source_target_pairs={{0,16},{16,0},{1,17},{17,1},{2,18},{18,2},{3,19},{19,3},{4,20},{20... | collective-permute-start | bytes 393224 | tf_op jit(solution)/shard_map/ppermute | solution.py:32
  428.9 10.2 %collective-permute-start.16 = (bf16[256,768]{1,0:T(8,128)(2,1)S(1)}, bf16[256,768]{1,0:T(8,128)(2,1)S(1)}, u32[]{:S(2)}, u32[]{:S(2)}) collective-permute-start(bf16[256,768]{1,0:T(8,128)(2,1)S(1)} %fusion.29), channel_id=1, source_target_pairs={{0,16},{16,0},{1,17},{17,1},{2,18},{18,2},{3,19},{19,3},{4,20},{20... | collective-permute-start | bytes 1179656 | tf_op jit(solution)/shard_map/ppermute | solution.py:32
  455.4 4.5 collective-permute-start.13
  (42 other events, 892.0 us)
Sparse Core Ops, SparseCore 0:
  22.9 47.6 all-gather.6
  84.5 42.5 reduce-scatter.4
  131.2 45.2 all-gather.8
  178.5 44.6 all-gather.10
  237.7 42.5 reduce-scatter.8
  282.5 43.1 reduce-scatter.6
  331.1 45.2 all-gather.12
  396.3 42.6 reduce-scatter.10
